TPU v7x, 32 devices: a whole 2x2x4 slice. The times are simulated.
32 devices in a mesh: row: 4 (over y, x), col: 8 (over z, core).
Axes of the slice: x: 2, y: 2, z: 4, core: 2. Of those that a mesh axis runs over, the one named last changes fastest.
Arguments:
- tensor: float32 [2048, 8192], P('row', 'col'), may hold values from -60 to 60, as said below
- factor: float32 [2048, 256], P('row'), may hold values from -0.125 to 0.125
Outputs:
- gram: float32 [2048, 2048], P('col', 'row')
- core: float32 [256, 8192], P('row', 'col')
Inputs may be any that keep to these rules, and one draw needn't show every extreme that they name: `tensor`: values of the unfolded field.
All inputs are finite; a program needn't handle non-finite values.
Results may differ from a plain program's by a relative error of at most 0.000096.
Values sent between devices are 32-bit elements; how exact they have to be, the bound alone decides.
No kernel may reach another device: no remote copies, remote signals or barrier semaphores. Data moves between devices by JAX's collectives and lax.ppermute only.
A program may use at most 64 MiB of HBM per device.

v0:
```python
import jax
import jax.numpy as jnp
from jax import lax
from jax.sharding import PartitionSpec as P


def product(left, right_rows):
    return lax.dot_general(
        left,
        right_rows,
        (((1,), (1,)), ((), ())),
        precision=lax.Precision.HIGHEST,
        preferred_element_type=jnp.float32,
    )


def project(columns, slabs):
    return lax.dot_general(
        columns,
        slabs,
        (((0,), (0,)), ((), ())),
        precision=lax.Precision.HIGHEST,
        preferred_element_type=jnp.float32,
    )


def body(tensor, factor):
    col_count = lax.axis_size("col")
    inverse = 1.0 / (tensor.shape[1] * col_count)
    gathered = lax.all_gather(tensor, "row", axis=0, tiled=True)
    gram = lax.psum_scatter(
        product(gathered, tensor) * inverse, "col", scatter_dimension=0, tiled=True
    )
    core_rows = lax.psum_scatter(project(factor, tensor), "row", scatter_dimension=0, tiled=True)
    return (gram, core_rows)


def solution(mesh):
    placed = (P("row", "col"), P("row", None))
    return jax.shard_map(
        body,
        mesh=mesh,
        in_specs=placed,
        out_specs=(P("col", "row"), P("row", "col")),
        check_vma=False,
    )
```

profile of v0, /device:TPU:0, one launch (start us, length us, event | category | flops | bytes accessed | tf_op | source)
XLA Modules:
  0.0 191.0 jit_solution(983064396208909490)
XLA Ops:
  7.2 0.0 copy-start
  7.2 0.0 copy-start.1
  7.2 0.0 all-gather.2.cloned.1.call-start
  7.2 0.7 all-gather.2.cloned.1.call-update
  7.9 0.0 reduce-scatter.5.cloned.1.call-start
  8.0 0.2 copy-done
  8.2 4.5 %fusion = f32[256,1024]{1,0:T(8,128)} fusion(f32[512,256]{1,0:T(8,128)S(1)} %copy-done, f32[512,1024]{1,0:T(8,128)} %param.2), kind=kOutput, calls=%fused_computation.1 | convolution fusion | flops 1610612736 | bytes 3670016 | tf_op jit(solution)/shard_map/dot_general | solution.py:18
  12.7 0.0 reduce-scatter.5.cloned.1.call-update
  12.7 0.0 reduce-scatter.3.cloned.1.call-start
  12.8 87.4 %all-gather.2.cloned.1.call-done = f32[2048,1024]{1,0:T(8,128)} async-done(((f32[512,1024]{1,0:T(8,128)}), f32[2048,1024]{1,0:T(8,128)}) %all-gather.2.cloned.1.call-update) | async-done | bytes 8388624 | tf_op jit(solution)/shard_map/all_gather | solution.py:30
  100.2 0.0 copy-done.1
  100.2 16.9 %convolution_multiply_fusion = f32[2048,512]{1,0:T(8,128)} fusion(f32[2048,1024]{1,0:T(8,128)} %all-gather.2.cloned.1.call-done, f32[512,1024]{1,0:T(8,128)S(1)} %copy-done.1), kind=kOutput, calls=%fused_computation | convolution fusion | flops 12885950464 | bytes 14680064 | tf_op jit(solution)/shard_map/dot_general | solution.py:8
  117.1 0.0 reduce-scatter.3.cloned.1.call-update
  117.2 14.3 %reduce-scatter.5.cloned.1.call-done = f32[64,1024]{1,0:T(8,128)} async-done(((f32[256,1024]{1,0:T(8,128)}), f32[64,1024]{1,0:T(8,128)}) %reduce-scatter.5.cloned.1.call-update) | async-done | bytes 262160 | tf_op jit(solution)/shard_map/reduce_scatter | solution.py:34
  131.4 53.0 %reduce-scatter.3.cloned.1.call-done = f32[256,512]{1,0:T(8,128)} async-done(((f32[2048,512]{1,0:T(8,128)}), f32[256,512]{1,0:T(8,128)}) %reduce-scatter.3.cloned.1.call-update) | async-done | bytes 524304 | tf_op jit(solution)/shard_map/reduce_scatter | solution.py:31
Async XLA Ops:
  7.2 1.0 copy-start
  7.2 93.0 %copy-start.1 = (f32[512,1024]{1,0:T(8,128)S(1)}, f32[512,1024]{1,0:T(8,128)}, u32[]{:S(2)}) copy-start(f32[512,1024]{1,0:T(8,128)} %param.2) | copy-start | bytes 6291460
  7.2 93.0 %all-gather.2.cloned.1.call-start = ((), (), s32[]{:S(2)}) async-start(), calls=%async_computation.2 | async-start | bytes 10485760 | tf_op jit(solution)/shard_map/all_gather | solution.py:30
  7.9 123.5 %reduce-scatter.5.cloned.1.call-start = ((), (), s32[]{:S(2)}) async-start(), calls=%async_computation.4 | async-start | bytes 1310720 | tf_op jit(solution)/shard_map/reduce_scatter | solution.py:34
  12.7 171.7 %reduce-scatter.3.cloned.1.call-start = ((), (), s32[]{:S(2)}) async-start(), calls=%async_computation.3 | async-start | bytes 4718592 | tf_op jit(solution)/shard_map/reduce_scatter | solution.py:31
Sparse Core Ops, SparseCore 0:
  9.9 90.2 all-gather.1
  103.7 27.7 reduce-scatter.4
  134.4 49.9 reduce-scatter.2
where the time goes:
time: 191 us
  waiting for transfers between devices  155 us (81%)
  matrix products  21.4 us (11%)
  between operations  13.8 us (7%)
    all_gather x1, waiting for transfers between devices, body(): gathered = lax.all_gather(tensor, 'row', axis=0, tiled=True)  87.4 us
    reduce_scatter x1, waiting for transfers between devices, body(): lax.psum_scatter(product(gathered, tensor) * inverse, 'col', scatter_dime...  53 us
    dot_general x1, matrix products, product(): lax.dot_general(left, right_rows, (((1,), (1,)), ((), ())), precision=lax...  16.9 us
    reduce_scatter x1, waiting for transfers between devices, body(): lax.psum_scatter(project(factor, tensor), 'row', scatter_dimension=0, til...  14.3 us
    dot_general x1, matrix products, project(): lax.dot_general(columns, slabs, (((0,), (0,)), ((), ())), precision=lax.P...  4.48 us
  transfers between devices with their start and end apart: 3, of which 3 were waited for; matrix products, arithmetic and copies ran while one was open for 11% of the time, Pallas kernels for 0%

commit v1 on v0

v1 whole, which is shorter than its diff:
```python
import jax
import jax.numpy as jnp
import numpy as np
from jax import lax
from jax.sharding import PartitionSpec as P

AXES = ("row", "col")
CORES = 2


def contract_last(left, right):
    return lax.dot_general(
        left,
        right,
        (((1,), (1,)), ((), ())),
        precision=lax.Precision.HIGHEST,
        preferred_element_type=jnp.float32,
    )


def multiply(left, right):
    return lax.dot_general(
        left,
        right,
        (((1,), (0,)), ((), ())),
        precision=lax.Precision.HIGHEST,
        preferred_element_type=jnp.float32,
    )


class Layout:
    def __init__(self, rows, cols):
        self.rows, self.cols, self.chips = rows, cols, cols // CORES
        assert rows % 2 == 0 and cols % CORES == 0 and self.chips % rows == 0
        self.subs = self.chips // rows
        self.ring = [*range(0, rows, 2), *reversed(range(1, rows, 2))]
        self.place = {r: i for i, r in enumerate(self.ring)}
        self.devices = [(r, z, c) for r in range(rows) for z in range(self.chips) for c in range(CORES)]

    def flat(self, r, z, c):
        return r * self.cols + z * CORES + c

    def along(self, r, c, steps):
        return self.ring[(self.place[r] + (steps if c == 0 else -steps)) % self.rows]

    def swap(self):
        return [(self.flat(r, z, c), self.flat(r, z, 1 - c)) for r, z, c in self.devices]

    def fetch(self, steps):
        return [(self.flat(self.along(r, c, steps), z, c), self.flat(r, z, c)) for r, z, c in self.devices]

    def keeper(self, first, size, target):
        last = min(first + size, self.chips) - 1
        return min(max(target, first), last)

    def sums(self, steps, sub):
        rounds = []
        size = 1
        while size < self.chips:
            pairs = []
            for r in range(self.rows):
                for c in range(CORES):
                    target = self.along(r, c, steps) * self.subs + sub
                    for first in range(0, self.chips, 2 * size):
                        if first + size >= self.chips:
                            continue
                        a = self.keeper(first, size, target)
                        b = self.keeper(first + size, size, target)
                        to = self.keeper(first, 2 * size, target)
                        pairs.append((self.flat(r, a + b - to, c), self.flat(r, to, c)))
            rounds.append(pairs)
            size *= 2
        return rounds

    def classes(self):
        table = np.zeros((self.rows, self.cols), np.int32)
        for r, z, c in self.devices:
            ahead = self.place[z // self.subs] - self.place[r]
            table[r, z * CORES + c] = (ahead if c == 0 else -ahead) % self.rows
        return table


def body(tensor, factor):
    layout = Layout(lax.axis_size("row"), lax.axis_size("col"))
    rows, subs = layout.rows, layout.subs
    block, width = tensor.shape
    inverse = 1.0 / (width * layout.cols)
    row, col = lax.axis_index("row"), lax.axis_index("col")
    core = lax.rem(col, CORES)
    part = block // (subs * CORES)
    half = subs * part

    def send(value, pairs):
        return lax.ppermute(value, AXES, pairs)

    def my_rows(value):
        split = value.reshape(subs, CORES, part, value.shape[1])
        return lax.dynamic_index_in_dim(split, core, 1, keepdims=False).reshape(half, value.shape[1])

    def add_up(value, steps, sub):
        for pairs in layout.sums(steps, sub):
            value = value + send(value, pairs)
        return value

    near = my_rows(tensor)
    other = send(tensor, layout.swap())
    far = my_rows(other)

    def grams(near_rows, far_rows):
        return contract_last(near_rows, tensor) + contract_last(far_rows, other)

    forward, backward = rows // 2, (rows - 1) // 2
    blocks = {0: (near, far)}
    last = forward
    for steps in range(1, forward):
        before = blocks[steps - 1]
        blocks[steps] = tuple(send(b, layout.fetch(1)) for b in before)
    for steps in range(1, backward + 1):
        before = blocks[(rows - steps + 1) % rows]
        blocks[rows - steps] = tuple(send(b, layout.fetch(-1)) for b in before)

    both = jnp.concatenate(blocks[last - 1], axis=1).reshape(subs, part, 2 * width)
    cuts = [0, part // 2, part * 3 // 4, part]
    pieces = [
        send(both[:, a:b].reshape(subs * (b - a), 2 * width), layout.fetch(1)) for a, b in zip(cuts, cuts[1:])
    ]

    summed = {}
    for steps, (n, f) in blocks.items():
        product = grams(n, f).reshape(subs, part, block)
        summed[steps] = [add_up(product[s], steps, s) for s in range(subs)]
    tail = []
    for piece in pieces:
        product = grams(piece[:, :width], piece[:, width:]).reshape(subs, -1, block)
        tail.append([add_up(product[s], last, s) for s in range(subs)])
    summed[last] = [jnp.concatenate([t[s] for t in tail], axis=0) for s in range(subs)]

    kind = jnp.asarray(layout.classes())[row, col]
    sub = lax.rem(col // CORES, subs)
    gram = jnp.zeros((part, block), jnp.float32)
    for steps, values in summed.items():
        for s, value in enumerate(values):
            gram = jnp.where((kind == steps) & (sub == s), value, gram)
    gram = gram * inverse

    rank = factor.shape[1] // rows
    columns = my_rows(factor).T.reshape(rows, rank, half)
    ring = jnp.asarray(np.array([[[layout.along(r, c, s) for s in range(rows)] for c in range(CORES)] for r in range(rows)]))
    total = None
    for steps in range(rows):
        mine = lax.dynamic_index_in_dim(columns, ring[row, core, (rows - steps) % rows], 0, keepdims=False)
        weights = send(mine, layout.fetch(steps)) if steps else mine
        if steps == last:
            share = 0.0
            weights = weights.reshape(rank, subs, part)
            for (a, b), piece in zip(zip(cuts, cuts[1:]), pieces):
                share = share + multiply(weights[:, :, a:b].reshape(rank, -1), piece)
            near_share, far_share = share[:, :width], share[:, width:]
        else:
            near_share, far_share = (multiply(weights, b) for b in blocks[steps])
        total = (near_share, far_share) if total is None else (total[0] + near_share, total[1] + far_share)
    core_rows = total[0] + send(total[1], layout.swap())
    return (gram, core_rows)


def solution(mesh):
    placed = (P("row", "col"), P("row", None))
    return jax.shard_map(
        body,
        mesh=mesh,
        in_specs=placed,
        out_specs=(P("col", "row"), P("row", "col")),
        check_vma=False,
    )
```

time: 191 us -> 151 us (0.79)
  the two profiles are of different devices: /device:TPU:0 before, /device:TPU:6 now
where the time goes in v1:
time: 151 us; the launch traced here: 150 us
  matrix products  51.7 us (34%)
  waiting for transfers between devices  42.2 us (28%)
  starting transfers between devices  30.9 us (20%)
  between operations  11.1 us (7%)
  local copies, waits for them, and re-layouts  9.41 us (6%)
  other arithmetic  4.35 us (3%)
    ppermute x24, waiting for transfers between devices, send(): return lax.ppermute(value, AXES, pairs)  42.2 us
    dot_general x12, matrix products, contract_last(): lax.dot_general(left, right, (((1,), (1,)), ((), ())), precision=lax.Prec...  38.5 us
    ppermute x24, starting transfers between devices, send(): return lax.ppermute(value, AXES, pairs)  30.9 us
    dot_general x9, matrix products, multiply(): lax.dot_general(left, right, (((1,), (0,)), ((), ())), precision=lax.Prec...  13.2 us
    reshape x2, local copies, waits for them, and re-layouts, my_rows(): lax.dynamic_index_in_dim(split, core, 1, keepdims=False)  4.79 us
  transfers between devices with their start and end apart: 24, of which 10 were waited for; matrix products, arithmetic and copies ran while one was open for 43% of the time, Pallas kernels for 0%

profile of v1, /device:TPU:6, one launch (start us, length us, event | category | flops | bytes accessed | tf_op | source)
XLA Modules:
  0.0 149.6 jit_solution(11134299290578342038)
XLA Ops:
  0.7 2.4 %dynamic-slice_bitcast_fusion.1 = f32[256,1024]{1,0:T(8,128)} fusion(f32[1,2,256,1024]{3,2,1,0:T(8,128)} %bitcast.81, s32[]{:T(128)S(6)} %select_n.66), kind=kLoop, calls=%fused_computation.18 | loop fusion | bytes 2097156 | tf_op jit(solution)/shard_map/reshape | solution.py:98
  5.2 2.3 %dynamic-slice_bitcast_fusion = f32[256,1024]{1,0:T(8,128)} fusion(f32[1,2,256,1024]{3,2,1,0:T(8,128)} %bitcast.3, s32[]{:T(128)S(6)} %select_n.66), kind=kLoop, calls=%fused_computation.17 | loop fusion | bytes 2097156 | tf_op jit(solution)/shard_map/reshape | solution.py:98
  8.1 3.2 %fusion.25 = f32[256,512]{1,0:T(8,128)S(1)} fusion(f32[256,1024]{1,0:T(8,128)} %dynamic-slice_bitcast_fusion.1, f32[512,1024]{1,0:T(8,128)S(1)} %copy-done.1), kind=kOutput, calls=%fused_computation.54 | convolution fusion | flops 1610612736 | bytes 3670016 | tf_op jit(solution)/shard_map/dot_general | solution.py:12
  11.3 3.9 %convolution_add_fusion.1 = f32[256,512]{1,0:T(8,128)S(1)} fusion(f32[256,512]{1,0:T(8,128)S(1)} %fusion.25, f32[256,1024]{1,0:T(8,128)} %dynamic-slice_bitcast_fusion, f32[512,1024]{1,0:T(8,128)} %collective-permute-done.1), kind=kOutput, calls=%fused_computation.3 | convolution fusion | flops 1610743808 | bytes 4194304 | tf_op jit(solution)/shard_map/dot_general | solution.py:12
  15.1 4.3 %collective-permute-start.18 = (f32[256,512]{1,0:T(8,128)S(1)}, f32[256,512]{1,0:T(8,128)}, u32[]{:S(2)}, u32[]{:S(2)}) collective-permute-start(f32[256,512]{1,0:T(8,128)S(1)} %convolution_add_fusion.1), channel_id=1, source_target_pairs={{2,0},{6,4},{3,1},{7,5},{8,10},{14,12},{9,11},{15,13},{16,18},{22,... | collective-permute-start | bytes 1572872 | tf_op jit(solution)/shard_map/ppermute | solution.py:94
  41.2 3.9 %fusion.24 = f32[256,512]{1,0:T(8,128)S(1)} fusion(f32[256,1024]{1,0:T(8,128)} %collective-permute-done.2, f32[512,1024]{1,0:T(8,128)} %collective-permute-done.1), kind=kOutput, calls=%fused_computation.53 | convolution fusion | flops 1610612736 | bytes 3670016 | tf_op jit(solution)/shard_map/dot_general | solution.py:12
  46.6 3.2 %convolution_add_fusion.2 = f32[256,512]{1,0:T(8,128)S(1)} fusion(f32[256,512]{1,0:T(8,128)S(1)} %fusion.24, f32[256,1024]{1,0:T(8,128)} %collective-permute-done, f32[512,1024]{1,0:T(8,128)S(1)} %copy-done.1), kind=kOutput, calls=%fused_computation.4 | convolution fusion | flops 1610743808 | bytes 4194304 | tf_op jit(solution)/shard_map/dot_general | solution.py:12
  51.7 8.4 %collective-permute-done.13 = f32[256,1024]{1,0:T(8,128)S(1)} collective-permute-done((f32[256,1024]{1,0:T(8,128)}, f32[256,1024]{1,0:T(8,128)S(1)}, u32[]{:S(2)}, u32[]{:S(2)}) %collective-permute-start.13) | collective-permute-done | bytes 1048608 | tf_op jit(solution)/shard_map/ppermute | solution.py:94
  61.1 3.5 %fusion.23 = f32[256,512]{1,0:T(8,128)S(1)} fusion(f32[256,1024]{1,0:T(8,128)S(1)} %collective-permute-done.13, f32[512,1024]{1,0:T(8,128)} %collective-permute-done.1), kind=kOutput, calls=%fused_computation.52 | convolution fusion | flops 1610612736 | bytes 3670016 | tf_op jit(solution)/shard_map/dot_general | solution.py:12
  69.3 3.2 %convolution_add_fusion.3 = f32[256,512]{1,0:T(8,128)S(1)} fusion(f32[256,512]{1,0:T(8,128)S(1)} %fusion.23, f32[256,1024]{1,0:T(8,128)} %collective-permute-done.12, f32[512,1024]{1,0:T(8,128)S(1)} %copy-done.1), kind=kOutput, calls=%fused_computation.5 | convolution fusion | flops 1610743808 | bytes 4194304 | tf_op jit(solution)/shard_map/dot_general | solution.py:12
  72.4 2.5 %collective-permute-done.6 = f32[64,2048]{1,0:T(8,128)S(1)} collective-permute-done((f32[64,2048]{1,0:T(8,128)S(1)}, f32[64,2048]{1,0:T(8,128)S(1)}, u32[]{:S(2)}, u32[]{:S(2)}) %collective-permute-start.6) | collective-permute-done | bytes 524320 | tf_op jit(solution)/shard_map/ppermute | solution.py:94
  74.9 4.7 %collective-permute-start.14 = (f32[256,512]{1,0:T(8,128)S(1)}, f32[256,512]{1,0:T(8,128)S(1)}, u32[]{:S(2)}, u32[]{:S(2)}) collective-permute-start(f32[256,512]{1,0:T(8,128)S(1)} %convolution_add_fusion.3), channel_id=1, source_target_pairs={{0,2},{6,4},{1,3},{7,5},{8,10},{12,14},{11,9},{15,13},{18,16},{22,... | collective-permute-start | bytes 1572872 | tf_op jit(solution)/shard_map/ppermute | solution.py:94
  79.6 3.7 %fusion.11 = f32[64,512]{1,0:T(8,128)S(1)} fusion(f32[512,1024]{1,0:T(8,128)} %collective-permute-done.1, f32[64,2048]{1,0:T(8,128)S(1)} %collective-permute-done.6), kind=kOutput, calls=%fused_computation.29 | convolution fusion | flops 402653184 | bytes 2490368 | tf_op jit(solution)/shard_map/dot_general | solution.py:12
  86.8 3.7 %fusion.8 = f32[64,512]{1,0:T(8,128)S(1)} fusion(f32[512,1024]{1,0:T(8,128)} %collective-permute-done.1, f32[64,2048]{1,0:T(8,128)S(1)} %collective-permute-done.9), kind=kOutput, calls=%fused_computation.26 | convolution fusion | flops 402653184 | bytes 2490368 | tf_op jit(solution)/shard_map/dot_general | solution.py:12
  93.4 4.1 %collective-permute-done.16 = f32[256,512]{1,0:T(8,128)S(1)} collective-permute-done((f32[256,512]{1,0:T(8,128)S(1)}, f32[256,512]{1,0:T(8,128)S(1)}, u32[]{:S(2)}, u32[]{:S(2)}) %collective-permute-start.16) | collective-permute-done | bytes 524320 | tf_op jit(solution)/shard_map/ppermute | solution.py:94
  101.0 3.3 %collective-permute-done.7 = f32[64,512]{1,0:T(8,128)S(1)} collective-permute-done((f32[64,512]{1,0:T(8,128)S(1)}, f32[64,512]{1,0:T(8,128)S(1)}, u32[]{:S(2)}, u32[]{:S(2)}) %collective-permute-start.7) | collective-permute-done | bytes 131104 | tf_op jit(solution)/shard_map/ppermute | solution.py:94
  105.7 2.9 %collective-permute-done.10 = f32[64,512]{1,0:T(8,128)S(1)} collective-permute-done((f32[64,512]{1,0:T(8,128)S(1)}, f32[64,512]{1,0:T(8,128)S(1)}, u32[]{:S(2)}, u32[]{:S(2)}) %collective-permute-start.10) | collective-permute-done | bytes 131104 | tf_op jit(solution)/shard_map/ppermute | solution.py:94
  110.5 3.1 %collective-permute-done.8 = f32[64,512]{1,0:T(8,128)S(1)} collective-permute-done((f32[64,512]{1,0:T(8,128)S(1)}, f32[64,512]{1,0:T(8,128)S(1)}, u32[]{:S(2)}, u32[]{:S(2)}) %collective-permute-start.8) | collective-permute-done | bytes 131104 | tf_op jit(solution)/shard_map/ppermute | solution.py:94
  114.3 2.3 %collective-permute-done.11 = f32[64,512]{1,0:T(8,128)S(1)} collective-permute-done((f32[64,512]{1,0:T(8,128)S(1)}, f32[64,512]{1,0:T(8,128)S(1)}, u32[]{:S(2)}, u32[]{:S(2)}) %collective-permute-start.11) | collective-permute-done | bytes 131104 | tf_op jit(solution)/shard_map/ppermute | solution.py:94
  120.9 3.8 %fusion.4 = f32[128,512]{1,0:T(8,128)S(1)} fusion(f32[512,1024]{1,0:T(8,128)} %collective-permute-done.1, f32[128,2048]{1,0:T(8,128)S(1)} %collective-permute-done.3), kind=kOutput, calls=%fused_computation.21 | convolution fusion | flops 805306368 | bytes 2883584 | tf_op jit(solution)/shard_map/dot_general | solution.py:12
  124.7 2.2 %convolution_add_fusion.4 = f32[128,512]{1,0:T(8,128)S(1)} fusion(f32[128,512]{1,0:T(8,128)S(1)} %fusion.4, f32[512,1024]{1,0:T(8,128)S(1)} %copy-done.1, f32[128,2048]{1,0:T(8,128)S(1)} %collective-permute-done.3), kind=kOutput, calls=%fused_computation.6 | convolution fusion | flops 805371904 | bytes 3145728 | tf_op jit(solution)/shard_map/dot_general | solution.py:12
  130.3 7.3 %collective-permute-done.4 = f32[128,512]{1,0:T(8,128)S(1)} collective-permute-done((f32[128,512]{1,0:T(8,128)S(1)}, f32[128,512]{1,0:T(8,128)S(1)}, u32[]{:S(2)}, u32[]{:S(2)}) %collective-permute-start.4) | collective-permute-done | bytes 262176 | tf_op jit(solution)/shard_map/ppermute | solution.py:94
  138.9 2.7 %fusion.2 = f32[64,1024]{1,0:T(8,128)} fusion(f32[64,1024]{1,0:T(8,128)S(1)} %collective-permute-done.23, f32[64,1024]{1,0:T(8,128)S(1)} %fusion.3, f32[64,256]{1,0:T(8,128)S(1)} %collective-permute-done.22, f32[256,1024]{1,0:T(8,128)} %collective-permute-done.12), kind=kOutput, calls=%fused_computation.11 | convolution fusion | flops 201457664 | bytes 1900544 | tf_op jit(solution)/shard_map/dot_general | solution.py:22
  141.6 6.7 %collective-permute-done.5 = f32[128,512]{1,0:T(8,128)S(1)} collective-permute-done((f32[128,512]{1,0:T(8,128)S(1)}, f32[128,512]{1,0:T(8,128)S(1)}, u32[]{:S(2)}, u32[]{:S(2)}) %collective-permute-start.5) | collective-permute-done | bytes 262176 | tf_op jit(solution)/shard_map/ppermute | solution.py:94
  (71 shorter events, 47.2 us)
Async XLA Ops:
  0.6 4.6 %collective-permute-start.1 = (f32[512,1024]{1,0:T(8,128)}, f32[512,1024]{1,0:T(8,128)}, u32[]{:S(2)}, u32[]{:S(2)}) collective-permute-start(f32[512,1024]{1,0:T(8,128)} %param.4), channel_id=1, source_target_pairs={{0,1},{1,0},{2,3},{3,2},{4,5},{5,4},{6,7},{7,6},{8,9},{9,8},{10,11... | collective-permute-start | bytes 6291464 | tf_op jit(solution)/shard_map/ppermute | solution.py:94
  3.2 41.8 %collective-permute-start = (f32[256,1024]{1,0:T(8,128)}, f32[256,1024]{1,0:T(8,128)}, u32[]{:S(2)}, u32[]{:S(2)}) collective-permute-start(f32[256,1024]{1,0:T(8,128)} %dynamic-slice_bitcast_fusion.1), channel_id=1, source_target_pairs={{16,0},{9,1},{18,2},{11,3},{20,4},{13,5},{22,6},{15,7},{0,8},{25,9... | collective-permute-start | bytes 3145736 | tf_op jit(solution)/shard_map/ppermute | solution.py:94
  7.6 32.5 %collective-permute-start.2 = (f32[256,1024]{1,0:T(8,128)}, f32[256,1024]{1,0:T(8,128)}, u32[]{:S(2)}, u32[]{:S(2)}) collective-permute-start(f32[256,1024]{1,0:T(8,128)} %dynamic-slice_bitcast_fusion), channel_id=1, source_target_pairs={{16,0},{9,1},{18,2},{11,3},{20,4},{13,5},{22,6},{15,7},{0,8},{25,9... | collective-permute-start | bytes 3145736 | tf_op jit(solution)/shard_map/ppermute | solution.py:94
  15.1 22.8 %collective-permute-start.18 = (f32[256,512]{1,0:T(8,128)S(1)}, f32[256,512]{1,0:T(8,128)}, u32[]{:S(2)}, u32[]{:S(2)}) collective-permute-start(f32[256,512]{1,0:T(8,128)S(1)} %convolution_add_fusion.1), channel_id=1, source_target_pairs={{2,0},{6,4},{3,1},{7,5},{8,10},{14,12},{9,11},{15,13},{16,18},{22,... | collective-permute-start | bytes 1572872 | tf_op jit(solution)/shard_map/ppermute | solution.py:94
  19.4 49.3 %collective-permute-start.12 = (f32[256,1024]{1,0:T(8,128)}, f32[256,1024]{1,0:T(8,128)}, u32[]{:S(2)}, u32[]{:S(2)}) collective-permute-start(f32[256,1024]{1,0:T(8,128)} %dynamic-slice_bitcast_fusion.1), channel_id=1, source_target_pairs={{8,0},{17,1},{10,2},{19,3},{12,4},{21,5},{14,6},{23,7},{24,8},{1,9... | collective-permute-start | bytes 3145736 | tf_op jit(solution)/shard_map/ppermute | solution.py:94
  29.9 69.0 %collective-permute-start.21 = (f32[64,256]{1,0:T(8,128)}, f32[64,256]{1,0:T(8,128)S(1)}, u32[]{:S(2)}, u32[]{:S(2)}) collective-permute-start(f32[64,256]{1,0:T(8,128)} %get-tuple-element.5), channel_id=1, source_target_pairs={{24,0},{25,1},{26,2},{27,3},{28,4},{29,5},{30,6},{31,7},{16,8},{17... | collective-permute-start | bytes 196616 | tf_op jit(solution)/shard_map/ppermute | solution.py:94
  37.9 26.7 %collective-permute-start.20 = (f32[64,256]{1,0:T(8,128)}, f32[64,256]{1,0:T(8,128)S(1)}, u32[]{:S(2)}, u32[]{:S(2)}) collective-permute-start(f32[64,256]{1,0:T(8,128)} %get-tuple-element.6), channel_id=1, source_target_pairs={{16,0},{9,1},{18,2},{11,3},{20,4},{13,5},{22,6},{15,7},{0,8},{25,9... | collective-permute-start | bytes 196616 | tf_op jit(solution)/shard_map/ppermute | solution.py:94
  40.1 80.0 %collective-permute-start.22 = (f32[64,256]{1,0:T(8,128)S(1)}, f32[64,256]{1,0:T(8,128)S(1)}, u32[]{:S(2)}, u32[]{:S(2)}) collective-permute-start(f32[64,256]{1,0:T(8,128)S(1)} %get-tuple-element.4), channel_id=1, source_target_pairs={{8,0},{17,1},{10,2},{19,3},{12,4},{21,5},{14,6},{23,7},{24,8},{1,9... | collective-permute-start | bytes 196616 | tf_op jit(solution)/shard_map/ppermute | solution.py:94
  45.0 15.1 %collective-permute-start.13 = (f32[256,1024]{1,0:T(8,128)}, f32[256,1024]{1,0:T(8,128)S(1)}, u32[]{:S(2)}, u32[]{:S(2)}) collective-permute-start(f32[256,1024]{1,0:T(8,128)} %dynamic-slice_bitcast_fusion), channel_id=1, source_target_pairs={{8,0},{17,1},{10,2},{19,3},{12,4},{21,5},{14,6},{23,7},{24,8},{1,9... | collective-permute-start | bytes 3145736 | tf_op jit(solution)/shard_map/ppermute | solution.py:94
  60.1 25.4 %collective-permute-start.9 = (f32[64,2048]{1,0:T(8,128)S(1)}, f32[64,2048]{1,0:T(8,128)S(1)}, u32[]{:S(2)}, u32[]{:S(2)}) collective-permute-start(f32[64,2048]{1,0:T(8,128)S(1)} %get-tuple-element.3), channel_id=1, source_target_pairs={{16,0},{9,1},{18,2},{11,3},{20,4},{13,5},{22,6},{15,7},{0,8},{25,9... | collective-permute-start | bytes 1572872 | tf_op jit(solution)/shard_map/ppermute | solution.py:94
  64.7 10.3 %collective-permute-start.6 = (f32[64,2048]{1,0:T(8,128)S(1)}, f32[64,2048]{1,0:T(8,128)S(1)}, u32[]{:S(2)}, u32[]{:S(2)}) collective-permute-start(f32[64,2048]{1,0:T(8,128)S(1)} %get-tuple-element.2), channel_id=1, source_target_pairs={{16,0},{9,1},{18,2},{11,3},{20,4},{13,5},{22,6},{15,7},{0,8},{25,9... | collective-permute-start | bytes 1572872 | tf_op jit(solution)/shard_map/ppermute | solution.py:94
  68.7 48.7 %collective-permute-start.3 = (f32[128,2048]{1,0:T(8,128)S(1)}, f32[128,2048]{1,0:T(8,128)S(1)}, u32[]{:S(2)}, u32[]{:S(2)}) collective-permute-start(f32[128,2048]{1,0:T(8,128)S(1)} %slice_bitcast_fusion), channel_id=1, source_target_pairs={{16,0},{9,1},{18,2},{11,3},{20,4},{13,5},{22,6},{15,7},{0,8},{25,9... | collective-permute-start | bytes 3145736 | tf_op jit(solution)/shard_map/ppermute | solution.py:94
  74.9 17.7 %collective-permute-start.14 = (f32[256,512]{1,0:T(8,128)S(1)}, f32[256,512]{1,0:T(8,128)S(1)}, u32[]{:S(2)}, u32[]{:S(2)}) collective-permute-start(f32[256,512]{1,0:T(8,128)S(1)} %convolution_add_fusion.3), channel_id=1, source_target_pairs={{0,2},{6,4},{1,3},{7,5},{8,10},{12,14},{11,9},{15,13},{18,16},{22,... | collective-permute-start | bytes 1572872 | tf_op jit(solution)/shard_map/ppermute | solution.py:94
  85.5 12.0 %collective-permute-start.16 = (f32[256,512]{1,0:T(8,128)S(1)}, f32[256,512]{1,0:T(8,128)S(1)}, u32[]{:S(2)}, u32[]{:S(2)}) collective-permute-start(f32[256,512]{1,0:T(8,128)S(1)} %convolution_add_fusion.2), channel_id=1, source_target_pairs={{0,2},{6,4},{1,3},{7,5},{10,8},{14,12},{9,11},{13,15},{16,18},{20,... | collective-permute-start | bytes 1572872 | tf_op jit(solution)/shard_map/ppermute | solution.py:94
  92.7 55.7 %collective-permute-start.19 = (f32[256,512]{1,0:T(8,128)S(1)}, f32[256,512]{1,0:T(8,128)S(1)}, u32[]{:S(2)}, u32[]{:S(2)}) collective-permute-start(f32[256,512]{1,0:T(8,128)S(1)} %add.135), channel_id=1, source_target_pairs={{4,0},{5,1},{12,10},{13,11},{18,20},{19,21},{26,30},{27,31}} | collective-permute-start | bytes 1572872 | tf_op jit(solution)/shard_map/ppermute | solution.py:94
  97.5 6.8 %collective-permute-start.7 = (f32[64,512]{1,0:T(8,128)S(1)}, f32[64,512]{1,0:T(8,128)S(1)}, u32[]{:S(2)}, u32[]{:S(2)}) collective-permute-start(f32[64,512]{1,0:T(8,128)S(1)} %convolution_add_fusion.10), channel_id=1, source_target_pairs={{0,2},{4,6},{1,3},{5,7},{8,10},{14,12},{9,11},{15,13},{16,18},{22,... | collective-permute-start | bytes 393224 | tf_op jit(solution)/shard_map/ppermute | solution.py:94
  98.9 9.7 %collective-permute-start.10 = (f32[64,512]{1,0:T(8,128)S(1)}, f32[64,512]{1,0:T(8,128)S(1)}, u32[]{:S(2)}, u32[]{:S(2)}) collective-permute-start(f32[64,512]{1,0:T(8,128)S(1)} %convolution_add_fusion.9), channel_id=1, source_target_pairs={{0,2},{4,6},{1,3},{5,7},{8,10},{14,12},{9,11},{15,13},{16,18},{22,... | collective-permute-start | bytes 393224 | tf_op jit(solution)/shard_map/ppermute | solution.py:94
  104.4 9.2 %collective-permute-start.8 = (f32[64,512]{1,0:T(8,128)S(1)}, f32[64,512]{1,0:T(8,128)S(1)}, u32[]{:S(2)}, u32[]{:S(2)}) collective-permute-start(f32[64,512]{1,0:T(8,128)S(1)} %add.123), channel_id=1, source_target_pairs={{2,6},{3,7},{10,12},{11,13},{20,18},{21,19},{28,24},{29,25}} | collective-permute-start | bytes 393224 | tf_op jit(solution)/shard_map/ppermute | solution.py:94
  108.6 8.1 %collective-permute-start.11 = (f32[64,512]{1,0:T(8,128)S(1)}, f32[64,512]{1,0:T(8,128)S(1)}, u32[]{:S(2)}, u32[]{:S(2)}) collective-permute-start(f32[64,512]{1,0:T(8,128)S(1)} %add.126), channel_id=1, source_target_pairs={{2,6},{3,7},{10,12},{11,13},{20,18},{21,19},{28,24},{29,25}} | collective-permute-start | bytes 393224 | tf_op jit(solution)/shard_map/ppermute | solution.py:94
  113.6 34.8 %collective-permute-start.15 = (f32[256,512]{1,0:T(8,128)S(1)}, f32[256,512]{1,0:T(8,128)S(1)}, u32[]{:S(2)}, u32[]{:S(2)}) collective-permute-start(f32[256,512]{1,0:T(8,128)S(1)} %add.129), channel_id=1, source_target_pairs={{4,2},{3,5},{10,14},{13,9},{20,16},{19,23},{26,28},{29,27}} | collective-permute-start | bytes 1572872 | tf_op jit(solution)/shard_map/ppermute | solution.py:94
  116.6 31.8 %collective-permute-start.17 = (f32[256,512]{1,0:T(8,128)S(1)}, f32[256,512]{1,0:T(8,128)S(1)}, u32[]{:S(2)}, u32[]{:S(2)}) collective-permute-start(f32[256,512]{1,0:T(8,128)S(1)} %add.132), channel_id=1, source_target_pairs={{2,4},{5,3},{12,8},{11,15},{18,22},{21,17},{28,26},{27,29}} | collective-permute-start | bytes 1572872 | tf_op jit(solution)/shard_map/ppermute | solution.py:94
  120.8 18.1 %collective-permute-start.23 = (f32[64,1024]{1,0:T(8,128)S(1)}, f32[64,1024]{1,0:T(8,128)S(1)}, u32[]{:S(2)}, u32[]{:S(2)}) collective-permute-start(f32[64,1024]{1,0:T(8,128)S(1)} %convolution_add_fusion.5), channel_id=1, source_target_pairs={{0,1},{1,0},{2,3},{3,2},{4,5},{5,4},{6,7},{7,6},{8,9},{9,8},{10,11... | collective-permute-start | bytes 786440 | tf_op jit(solution)/shard_map/ppermute | solution.py:94
  127.0 10.6 %collective-permute-start.4 = (f32[128,512]{1,0:T(8,128)S(1)}, f32[128,512]{1,0:T(8,128)S(1)}, u32[]{:S(2)}, u32[]{:S(2)}) collective-permute-start(f32[128,512]{1,0:T(8,128)S(1)} %convolution_add_fusion.4), channel_id=1, source_target_pairs={{0,2},{4,6},{1,3},{5,7},{8,10},{14,12},{9,11},{15,13},{16,18},{22,... | collective-permute-start | bytes 786440 | tf_op jit(solution)/shard_map/ppermute | solution.py:94
  137.6 10.7 %collective-permute-start.5 = (f32[128,512]{1,0:T(8,128)S(1)}, f32[128,512]{1,0:T(8,128)S(1)}, u32[]{:S(2)}, u32[]{:S(2)}) collective-permute-start(f32[128,512]{1,0:T(8,128)S(1)} %add.120), channel_id=1, source_target_pairs={{2,6},{3,7},{10,12},{11,13},{20,18},{21,19},{28,24},{29,25}} | collective-permute-start | bytes 786440 | tf_op jit(solution)/shard_map/ppermute | solution.py:94
  (3 other events, 41.9 us)

commit v2 on v1

v2 whole, which is shorter than its diff:
```python
import functools

import jax
import jax.numpy as jnp
import numpy as np
from jax import lax
from jax.experimental import pallas as pl
from jax.experimental.pallas import tpu as pltpu
from jax.sharding import PartitionSpec as P

AXES = ("row", "col")
CORES = 2
FLOPS = 1_200_000_000
PARAMS = pltpu.CompilerParams(vmem_limit_bytes=40 * 2**20)


def shape(*dims, dtype=jnp.float32):
    return jax.ShapeDtypeStruct(dims, dtype)


class Layout:
    def __init__(self, rows, cols):
        self.rows, self.cols, self.chips = rows, cols, cols // CORES
        assert rows % 2 == 0 and cols % CORES == 0 and self.chips % rows == 0
        self.subs = self.chips // rows
        self.ring = [*range(0, rows, 2), *reversed(range(1, rows, 2))]
        self.place = {r: i for i, r in enumerate(self.ring)}
        self.devices = [(r, z, c) for r in range(rows) for z in range(self.chips) for c in range(CORES)]

    def flat(self, r, z, c):
        return r * self.cols + z * CORES + c

    def along(self, r, c, steps):
        return self.ring[(self.place[r] + (steps if c == 0 else -steps)) % self.rows]

    def swap(self):
        return [(self.flat(r, z, c), self.flat(r, z, 1 - c)) for r, z, c in self.devices]

    def fetch(self, steps):
        return [(self.flat(self.along(r, c, steps), z, c), self.flat(r, z, c)) for r, z, c in self.devices]

    def keeper(self, first, size, target):
        last = min(first + size, self.chips) - 1
        return min(max(target, first), last)

    def sums(self, steps, sub):
        rounds = []
        size = 1
        while size < self.chips:
            pairs = []
            for r in range(self.rows):
                for c in range(CORES):
                    target = self.along(r, c, steps) * self.subs + sub
                    for first in range(0, self.chips, 2 * size):
                        if first + size >= self.chips:
                            continue
                        a = self.keeper(first, size, target)
                        b = self.keeper(first + size, size, target)
                        to = self.keeper(first, 2 * size, target)
                        pairs.append((self.flat(r, a + b - to, c), self.flat(r, to, c)))
            rounds.append(pairs)
            size *= 2
        return rounds

    def classes(self):
        table = np.zeros((self.rows, self.cols), np.int32)
        for r, z, c in self.devices:
            ahead = self.place[z // self.subs] - self.place[r]
            table[r, z * CORES + c] = (ahead if c == 0 else -ahead) % self.rows
        return table

    def takers(self):
        return np.array(
            [[[self.along(r, c, -s) for s in range(self.rows)] for c in range(CORES)] for r in range(self.rows)],
            np.int32,
        )


def halves(value):
    high = value.astype(jnp.bfloat16)
    return high, (value - high.astype(jnp.float32)).astype(jnp.bfloat16)


def product(left, right, dims):
    def one(a, b):
        return lax.dot_general(a, b, (dims, ((), ())), preferred_element_type=jnp.float32)

    return one(left[0], right[0]) + (one(left[0], right[1]) + one(left[1], right[0]))


def call(kernel, outs, *args, name, flops=0, smem=0, scratch=()):
    vmem = pl.BlockSpec(memory_space=pltpu.VMEM)
    specs = [pl.BlockSpec(memory_space=pltpu.SMEM)] * smem + [vmem] * (len(args) - smem)
    return pl.pallas_call(
        kernel,
        out_shape=outs,
        in_specs=specs,
        out_specs=[vmem] * len(outs),
        scratch_shapes=list(scratch),
        compiler_params=PARAMS,
        cost_estimate=pl.CostEstimate(flops=flops, bytes_accessed=4 * sum(o.size for o in outs), transcendentals=0),
        name=name,
    )(*args)


def split_kernel(value, high, low):
    high[...], low[...] = halves(value[...])


def split(value):
    return call(split_kernel, [shape(*value.shape, dtype=jnp.bfloat16)] * 2, value, name="split")


class Extra:
    def __init__(self, count, rank, half, width):
        self.count, self.rank, self.half = count, rank, half
        self.folds = 1
        while 2 * self.folds * count * half <= width and rank % (32 * self.folds) == 0:
            self.folds *= 2
        self.height = rank // self.folds

    def lanes(self, fold, index):
        first = (fold * self.count + index) * self.half
        return slice(first, first + self.half)

    def write(self, out, first, index, matrix):
        for f in range(self.folds):
            out[first : first + self.height, self.lanes(f, index)] = matrix[f * self.height : (f + 1) * self.height]

    def read(self, rows, index):
        return jnp.concatenate([rows[:, self.lanes(f, index)] for f in range(self.folds)], axis=0)


def weights_kernel(subs, ahead, behind, where, factor, own, out_ahead, out_behind, turned):
    rank = ahead.rank
    part = factor.shape[0] // (subs * CORES)
    first = where[0] * part
    rows = [factor[pl.ds(pl.multiple_of(first + s * part * CORES, part), part), :] for s in range(subs)]
    turned[...] = jnp.concatenate(rows, axis=0).T

    def columns(steps):
        return turned[pl.ds(pl.multiple_of(where[1 + steps] * rank, rank), rank), :]

    own[...] = columns(0)
    for i in range(ahead.count):
        ahead.write(out_ahead, 0, i, columns(1 + i))
    for i in range(behind.count):
        behind.write(out_behind, 0, i, columns(ahead.count + behind.count - i))


def pack_kernel(subs, cuts, near, far, extra, *outs):
    width = near.shape[1]
    half = near.shape[0]
    part = half // subs
    for n, (a, b, out) in enumerate(zip(cuts, cuts[1:], outs)):
        for s in range(subs):
            out[s * (b - a) : (s + 1) * (b - a), :width] = near[s * part + a : s * part + b, :]
            out[s * (b - a) : (s + 1) * (b - a), width:] = far[s * part + a : s * part + b, :]
        if n == 0:
            height = extra.shape[0] // 2
            out[subs * (b - a) :, :width] = extra[:height, :]
            out[subs * (b - a) :, width:] = extra[height:, :]


def pack(subs, cuts, near, far, extra):
    width = near.shape[1]
    outs = [shape(subs * (b - a) + (extra.shape[0] // 2 if n == 0 else 0), 2 * width) for n, (a, b) in enumerate(zip(cuts, cuts[1:]))]
    return call(functools.partial(pack_kernel, subs, cuts), outs, near, far, extra, name="pack")


def step_kernel(extra, index, has_core, near, far, b0, b1, b2, b3, *refs):
    refs = list(refs)
    half = near.shape[0]
    weights = refs.pop(0)[...] if extra is None else extra.read(far[half:, :], index)
    core_in = [refs.pop(0), refs.pop(0)] if has_core else [None, None]
    gram, *core = refs
    weights = halves(weights)
    total = None
    for rows, high, low, old, new in ((near, b0, b1, core_in[0], core[0]), (far, b2, b3, core_in[1], core[1])):
        pair = halves(rows[:half, :])
        term = product(pair, (high[...], low[...]), ((1,), (1,)))
        total = term if total is None else total + term
        share = product(weights, pair, ((1,), (0,)))
        new[...] = old[...] + share if has_core else share
    gram[...] = total


def step(near, far, block, weights, rank, extra=None, index=None, core=()):
    outs = [shape(near.shape[0], block[0].shape[0])] + [shape(rank, near.shape[1])] * 2
    args = [near, far, *block, *([] if weights is None else [weights]), *core]
    out = call(functools.partial(step_kernel, extra, index, len(core) > 0), outs, *args, name="step", flops=2 * FLOPS)
    return out[0], out[1:]


def piece_kernel(rows, b0, b1, b2, b3, gram):
    count, width = gram.shape[0], b0.shape[1]
    left = product(halves(rows[:count, :width]), (b0[...], b1[...]), ((1,), (1,)))
    gram[...] = left + product(halves(rows[:count, width:]), (b2[...], b3[...]), ((1,), (1,)))


def piece_step(rows, count, block):
    return call(piece_kernel, [shape(count, block[0].shape[0])], rows, *block, name="piece", flops=FLOPS)[0]


def core_kernel(subs, cuts, extra, index, *refs):
    *pieces, old0, old1, new0, new1 = refs
    width = old0.shape[1]
    sizes = [b - a for a, b in zip(cuts, cuts[1:])]
    folded = pieces[0][subs * sizes[0] :, :]
    weights = halves(extra.read(jnp.concatenate([folded[:, :width], folded[:, width:]], axis=0), index))
    for lanes, old, new in ((slice(0, width), old0, new0), (slice(width, None), old1, new1)):
        rows = jnp.concatenate([p[s * n : (s + 1) * n, lanes] for s in range(subs) for p, n in zip(pieces, sizes)], axis=0)
        new[...] = old[...] + product(weights, halves(rows), ((1,), (0,)))


def core_step(subs, cuts, extra, index, pieces, core):
    outs = [shape(*c.shape) for c in core]
    return call(functools.partial(core_kernel, subs, cuts, extra, index), outs, *pieces, *core, name="core", flops=FLOPS // 2)


def finish_kernel(subs, cuts, inverse, counts, where, *refs):
    *refs, share, other_share, gram, core = refs
    kind, sub = where[0], where[1]
    core[...] = share[...] + other_share[...]
    refs = list(refs)
    for steps, count in counts:
        first = 0
        pieces = []
        for _ in range(count):
            for s in range(subs):
                value, received = refs.pop(0), refs.pop(0)
                pieces.append((s, first, value, received))
            first += value.shape[0]

        for s in range(subs):

            @pl.when((kind == steps) & (sub == s))
            def _(chosen=[p for p in pieces if p[0] == s]):
                for _, first, value, received in chosen:
                    gram[first : first + value.shape[0], :] = (value[...] + received[...]) * inverse


class Sums:
    def __init__(self, values, rounds, send):
        self.values, self.rounds, self.send, self.next, self.received = list(values), rounds, send, 0, []

    def advance(self):
        if self.next < len(self.rounds[0]):
            received = [self.send(v, r[self.next]) for v, r in zip(self.values, self.rounds)]
            self.next += 1
            if self.next < len(self.rounds[0]):
                self.values = [v + r for v, r in zip(self.values, received)]
            else:
                self.received = received
        return self

    def finish(self):
        for _ in self.rounds[0]:
            self.advance()

    def held(self):
        return self.received or self.values


def body(tensor, factor):
    layout = Layout(lax.axis_size("row"), lax.axis_size("col"))
    rows, subs = layout.rows, layout.subs
    block, width = tensor.shape
    inverse = 1.0 / (width * layout.cols)
    row, col = lax.axis_index("row"), lax.axis_index("col")
    core = lax.rem(col, CORES)
    part = block // (subs * CORES)
    half = subs * part
    rank = factor.shape[1] // rows

    def send(value, pairs):
        return lax.ppermute(value, AXES, pairs)

    arrived = []

    def fetch(value, steps, *work):
        names = [(arrived, len(arrived) - 2)] if len(arrived) >= 2 else []
        names += [(w.held(), i) for w in work for i in range(subs)]
        if names:
            value, *held = lax.optimization_barrier((value, *(a[i] for a, i in names)))
            for (a, i), h in zip(names, held):
                a[i] = h
        arrived.append(send(value, layout.fetch(steps)))
        return len(arrived) - 1

    def my_rows(value):
        split_rows = value.reshape(subs, CORES, part, value.shape[1])
        return lax.dynamic_index_in_dim(split_rows, core, 1, keepdims=False).reshape(half, value.shape[1])

    classes = {}

    def sums(gram, steps):
        found = Sums(gram.reshape(subs, -1, block), [layout.sums(steps, s) for s in range(subs)], send)
        classes.setdefault(steps, []).append(found)
        return found

    last = rows // 2
    ahead = Extra(last, rank, half, width)
    behind = Extra(rows - 1 - last, rank, half, width)

    near = my_rows(tensor)
    other = send(tensor, layout.swap())
    far = my_rows(other)

    near_row, near = lax.optimization_barrier((row, near))
    table = np.concatenate([np.repeat(layout.takers(), layout.chips, 1).reshape(rows, CORES, layout.chips, rows).swapaxes(1, 2).reshape(rows, layout.cols, rows), layout.classes()[:, :, None]], axis=2)
    found = lax.dynamic_slice(jnp.asarray(table), (near_row, col, 0), (1, 1, rows + 1)).reshape(rows + 1)
    where = jnp.concatenate([core[None].astype(jnp.int32), found])
    place = jnp.stack([found[rows], lax.rem(col // CORES, subs).astype(jnp.int32)])
    own, ride_ahead, ride_behind = call(
        functools.partial(weights_kernel, subs, ahead, behind),
        [shape(rank, half), shape(ahead.height, width), shape(behind.height, width)],
        where,
        factor,
        name="weights",
        smem=1,
        scratch=[pltpu.VMEM((factor.shape[1], half), jnp.float32)],
    )

    first = {1: (near, jnp.concatenate([far, ride_ahead], axis=0), 1), rows - 1: (near, jnp.concatenate([far, ride_behind], axis=0), -1)}
    order = [*range(1, last + 1), *range(rows - 1, last + 1, -1)]
    at = {}

    def got(steps):
        return tuple(arrived[i] for i in at[steps])

    def source(steps):
        if steps in first:
            return first[steps]
        return (*got(steps - 1), 1) if steps <= last else (*got(steps + 1), -1)

    def fetch_half(steps, which, *work):
        value = source(steps)
        at[steps] = (*at.get(steps, ()), fetch(value[which], value[2], *work))

    fetch_half(1, 0)
    fetch_half(1, 1)
    pair = [*split(tensor), *split(other)]
    gram, core_sums = step(near, far, pair, own, rank)
    fresh, older, before = sums(gram, 0), [], 1

    def work_on(steps):
        nonlocal core_sums
        extra, index = (ahead, steps - 1) if steps <= last else (behind, rows - 1 - steps)
        gram, core_sums = step(*got(steps), pair, None, rank, extra, index, core_sums)
        return sums(gram, steps)

    for steps in order[1:]:
        fetch_half(steps, 0, fresh)
        fetch_half(steps, 1)
        older.append(fresh.advance())
        fresh, before = work_on(before), steps

    cuts = [0, part // 2, part * 3 // 4, part]
    near_rows, far_rows, way = source(last + 1)
    p0, p1, p2 = pack(subs, cuts, near_rows, far_rows[:half], far_rows[half:])
    at_pieces = [fetch(p0, way, fresh, *older)]
    older.append(fresh)
    for f in older:
        f.advance()
    at_pieces.append(fetch(p1, way, *older))
    fresh = work_on(before)
    for f in older:
        f.advance()
    at_pieces.append(fetch(p2, way, fresh))
    for f in (*older, fresh):
        f.finish()
    for a, b, i in zip(cuts, cuts[1:], at_pieces):
        sums(piece_step(arrived[i], subs * (b - a), pair), last + 1).finish()

    share, other_share = core_step(subs, cuts, behind, behind.count - 1, [arrived[i] for i in at_pieces], core_sums)
    counts = [(steps, len(found)) for steps, found in classes.items()]
    sent = [x for found in classes.values() for f in found for pair in zip(f.values, f.received) for x in pair]
    return tuple(
        call(
            functools.partial(finish_kernel, subs, cuts, inverse, counts),
            [shape(part, block), shape(rank, width)],
            place,
            *sent,
            share,
            send(other_share, layout.swap()),
            name="finish",
            smem=1,
        )
    )


def solution(mesh):
    placed = (P("row", "col"), P("row", None))
    return jax.shard_map(
        body,
        mesh=mesh,
        in_specs=placed,
        out_specs=(P("col", "row"), P("row", "col")),
        check_vma=False,
    )
```

time: 151 us -> 108 us (0.72)
  the two profiles are of different devices: /device:TPU:6 before, /device:TPU:8 now
where the time goes in v2:
time: 108 us
  waiting for transfers between devices  52.6 us (49%)
  starting transfers between devices  30.3 us (28%)
  Pallas kernels  18.2 us (17%)
  local copies, waits for them, and re-layouts  4.4 us (4%)
  other arithmetic  1.23 us (1%)
    ppermute x21, waiting for transfers between devices, send(): return lax.ppermute(value, AXES, pairs)  52.6 us
    ppermute x21, starting transfers between devices, send(): return lax.ppermute(value, AXES, pairs)  30.3 us
    pallas_call x12, Pallas kernels, call(): pl.pallas_call(kernel, out_shape=outs, in_specs=specs, out_specs=[vmem] *...  18.2 us
  transfers between devices with their start and end apart: 21, of which 11 were waited for; matrix products, arithmetic and copies ran while one was open for 4% of the time, Pallas kernels for 16%

profile of v2, /device:TPU:8, one launch (start us, length us, event | category | flops | bytes accessed | tf_op | source)
XLA Modules:
  0.0 107.6 jit_solution(15691953761597512208)
XLA Ops:
  2.0 1.5 %collective-permute-start.1 = (f32[256,1024]{1,0:T(8,128)S(1)}, f32[256,1024]{1,0:T(8,128)}, u32[]{:S(2)}, u32[]{:S(2)}) collective-permute-start(f32[256,1024]{1,0:T(8,128)S(1)} %dynamic-slice_bitcast_fusion.1.near), channel_id=1, source_target_pairs={{16,0},{9,1},{18,2},{11,3},{20,4},{13,5},{22,6},{15,7},{0,8},{25,9... | collective-permute-start | bytes 3145736 | tf_op jit(solution)/shard_map/ppermute | solution.py:277
  6.3 1.6 %collective-permute-start.3 = (f32[288,1024]{1,0:T(8,128)S(1)}, f32[288,1024]{1,0:T(8,128)S(1)}, u32[]{:S(2)}, u32[]{:S(2)}) collective-permute-start(f32[288,1024]{1,0:T(8,128)S(1)} %pad_maximum_fusion), channel_id=1, source_target_pairs={{16,0},{9,1},{18,2},{11,3},{20,4},{13,5},{22,6},{15,7},{0,8},{25,9... | collective-permute-start | bytes 3538952 | tf_op jit(solution)/shard_map/ppermute | solution.py:277
  8.5 2.4 %step.3 = (f32[256,512]{1,0:T(8,128)S(1)}, f32[64,1024]{1,0:T(8,128)S(1)}, f32[64,1024]{1,0:T(8,128)S(1)}) custom-call(f32[256,1024]{1,0:T(8,128)S(1)} %dynamic-slice_bitcast_fusion.1.near, f32[256,1024]{1,0:T(8,128)S(1)} %dynamic-slice_bitcast_fusion.far, bf16[512,1024]{1,0:T(8,128)(2,1)S(1)} %get-tuple-element.45.b0, ...), custom_call_target="tpu_custom_call" | custom-call | flops 2400000000 | bytes 1048576 | tf_op jit(solution)/shard_map/step/pallas_call | solution.py:94
  10.9 6.1 %collective-permute-done.1.near = f32[256,1024]{1,0:T(8,128)} collective-permute-done((f32[256,1024]{1,0:T(8,128)S(1)}, f32[256,1024]{1,0:T(8,128)}, u32[]{:S(2)}, u32[]{:S(2)}) %collective-permute-start.1) | collective-permute-done | bytes 1048608 | tf_op jit(solution)/shard_map/ppermute | solution.py:277
  17.0 1.5 %collective-permute-start.2 = (f32[256,1024]{1,0:T(8,128)}, f32[256,1024]{1,0:T(8,128)S(1)}, u32[]{:S(2)}, u32[]{:S(2)}) collective-permute-start(f32[256,1024]{1,0:T(8,128)} %collective-permute-done.1.near), channel_id=1, source_target_pairs={{16,0},{9,1},{18,2},{11,3},{20,4},{13,5},{22,6},{15,7},{0,8},{25,9... | collective-permute-start | bytes 3145736 | tf_op jit(solution)/shard_map/ppermute | solution.py:277
  18.5 2.4 %collective-permute-start.4 = (f32[256,512]{1,0:T(8,128)S(1)}, f32[256,512]{1,0:T(8,128)S(1)}, u32[]{:S(2)}, u32[]{:S(2)}) collective-permute-start(f32[256,512]{1,0:T(8,128)S(1)} %get-tuple-element.58), channel_id=1, source_target_pairs={{2,0},{6,4},{3,1},{7,5},{8,10},{14,12},{9,11},{15,13},{16,18},{22,... | collective-permute-start | bytes 1572872 | tf_op jit(solution)/shard_map/ppermute | solution.py:277
  20.9 8.7 %collective-permute-done.3.far = f32[288,1024]{1,0:T(8,128)S(1)} collective-permute-done((f32[288,1024]{1,0:T(8,128)S(1)}, f32[288,1024]{1,0:T(8,128)S(1)}, u32[]{:S(2)}, u32[]{:S(2)}) %collective-permute-start.3) | collective-permute-done | bytes 1179680 | tf_op jit(solution)/shard_map/ppermute | solution.py:277
  31.6 3.6 %step.4 = (f32[256,512]{1,0:T(8,128)S(1)}, f32[64,1024]{1,0:T(8,128)S(1)}, f32[64,1024]{1,0:T(8,128)S(1)}) custom-call(f32[256,1024]{1,0:T(8,128)} %collective-permute-done.1.near, f32[288,1024]{1,0:T(8,128)S(1)} %collective-permute-done.3.far, bf16[512,1024]{1,0:T(8,128)(2,1)S(1)} %get-tuple-element.45.b0, bf16[512,1024]{1,0:T(8,128)(2,1)S(1)} %get-tuple-element.46.b1, ...), custom_call_target="tpu_custom_call" | custom-call | flops 2400000000 | bytes 1048576 | tf_op jit(solution)/shard_map/step/pallas_call | solution.py:94
  35.2 5.5 %collective-permute-done.2.near = f32[256,1024]{1,0:T(8,128)S(1)} collective-permute-done((f32[256,1024]{1,0:T(8,128)}, f32[256,1024]{1,0:T(8,128)S(1)}, u32[]{:S(2)}, u32[]{:S(2)}) %collective-permute-start.2) | collective-permute-done | bytes 1048608 | tf_op jit(solution)/shard_map/ppermute | solution.py:277
  40.8 1.5 %collective-permute-start.9 = (f32[136,2048]{1,0:T(8,128)S(1)}, f32[136,2048]{1,0:T(8,128)S(1)}, u32[]{:S(2)}, u32[]{:S(2)}) collective-permute-start(f32[136,2048]{1,0:T(8,128)S(1)} %get-tuple-element.66), channel_id=1, source_target_pairs={{8,0},{17,1},{10,2},{19,3},{12,4},{21,5},{14,6},{23,7},{24,8},{1,9... | collective-permute-start | bytes 3342344 | tf_op jit(solution)/shard_map/ppermute | solution.py:277
  44.3 13.0 %collective-permute-done.7 = f32[256,512]{1,0:T(8,128)S(1)} collective-permute-done((f32[256,512]{1,0:T(8,128)S(1)}, f32[256,512]{1,0:T(8,128)S(1)}, u32[]{:S(2)}, u32[]{:S(2)}) %collective-permute-start.7) | collective-permute-done | bytes 524320 | tf_op jit(solution)/shard_map/ppermute | solution.py:277
  57.4 6.3 %collective-permute-done.5.far = f32[288,1024]{1,0:T(8,128)S(1)} collective-permute-done((f32[288,1024]{1,0:T(8,128)S(1)}, f32[288,1024]{1,0:T(8,128)S(1)}, u32[]{:S(2)}, u32[]{:S(2)}) %collective-permute-start.5) | collective-permute-done | bytes 1179680 | tf_op jit(solution)/shard_map/ppermute | solution.py:277
  63.7 2.4 %step.5 = (f32[256,512]{1,0:T(8,128)S(1)}, f32[64,1024]{1,0:T(8,128)S(1)}, f32[64,1024]{1,0:T(8,128)S(1)}) custom-call(f32[256,1024]{1,0:T(8,128)S(1)} %collective-permute-done.2.near, f32[288,1024]{1,0:T(8,128)S(1)} %collective-permute-done.5.far, bf16[512,1024]{1,0:T(8,128)(2,1)S(1)} %get-tuple-element.45.b0, bf16[512,1024]{1,0:T(8,128)(2,1)S(1)} %get-tuple-element.46.b1, ...), custom_call_target="tpu_custom_call" | custom-call | flops 2400000000 | bytes 1048576 | tf_op jit(solution)/shard_map/step/pallas_call | solution.py:94
  67.5 1.6 %collective-permute-start.17 = (f32[64,2048]{1,0:T(8,128)S(1)}, f32[64,2048]{1,0:T(8,128)S(1)}, u32[]{:S(2)}, u32[]{:S(2)}) collective-permute-start(f32[64,2048]{1,0:T(8,128)S(1)} %get-tuple-element.75), channel_id=1, source_target_pairs={{8,0},{17,1},{10,2},{19,3},{12,4},{21,5},{14,6},{23,7},{24,8},{1,9... | collective-permute-start | bytes 1572872 | tf_op jit(solution)/shard_map/ppermute | solution.py:277
  69.0 2.6 %collective-permute-start.14 = (f32[64,2048]{1,0:T(8,128)S(1)}, f32[64,2048]{1,0:T(8,128)S(1)}, u32[]{:S(2)}, u32[]{:S(2)}) collective-permute-start(f32[64,2048]{1,0:T(8,128)S(1)} %get-tuple-element.74), channel_id=1, source_target_pairs={{8,0},{17,1},{10,2},{19,3},{12,4},{21,5},{14,6},{23,7},{24,8},{1,9... | collective-permute-start | bytes 1572872 | tf_op jit(solution)/shard_map/ppermute | solution.py:277
  71.6 2.4 %collective-permute-start.8 = (f32[256,512]{1,0:T(8,128)S(1)}, f32[256,512]{1,0:T(8,128)S(1)}, u32[]{:S(2)}, u32[]{:S(2)}) collective-permute-start(f32[256,512]{1,0:T(8,128)S(1)} %add.34.refs_2_), channel_id=1, source_target_pairs={{2,4},{5,3},{12,8},{11,15},{18,22},{21,17},{28,26},{27,29}} | collective-permute-start | bytes 1572872 | tf_op jit(solution)/shard_map/ppermute | solution.py:277
  74.0 2.2 %piece.3 = f32[128,512]{1,0:T(8,128)S(1)} custom-call(f32[136,2048]{1,0:T(8,128)S(1)} %collective-permute-done.9.rows.refs_0_, bf16[512,1024]{1,0:T(8,128)(2,1)S(1)} %get-tuple-element.45.b0, bf16[512,1024]{1,0:T(8,128)(2,1)S(1)} %get-tuple-element.46.b1, bf16[512,1024]{1,0:T(8,128)(2,1)S(1)} %get-tuple-element.47.b2, bf16[512,1024]{1,0:T(8,128)(2,1)S(1)} %get-tuple-element.48.b3), custom_call_target="tpu_custom_call" | custom-call | flops 1200000000 | bytes 262144 | tf_op jit(solution)/shard_map/piece/pallas_call | solution.py:94
  77.5 5.4 %collective-permute-done.10 = f32[256,512]{1,0:T(8,128)S(1)} collective-permute-done((f32[256,512]{1,0:T(8,128)S(1)}, f32[256,512]{1,0:T(8,128)S(1)}, u32[]{:S(2)}, u32[]{:S(2)}) %collective-permute-start.10) | collective-permute-done | bytes 524320 | tf_op jit(solution)/shard_map/ppermute | solution.py:277
  83.0 2.5 %collective-permute-start.11 = (f32[256,512]{1,0:T(8,128)S(1)}, f32[256,512]{1,0:T(8,128)S(1)}, u32[]{:S(2)}, u32[]{:S(2)}) collective-permute-start(f32[256,512]{1,0:T(8,128)S(1)} %add.35.refs_4_), channel_id=1, source_target_pairs={{2,6},{3,7},{10,12},{11,13},{20,18},{21,19},{28,24},{29,25}} | collective-permute-start | bytes 1572872 | tf_op jit(solution)/shard_map/ppermute | solution.py:277
  85.5 2.0 %piece.5 = f32[64,512]{1,0:T(8,128)S(1)} custom-call(f32[64,2048]{1,0:T(8,128)S(1)} %collective-permute-done.17.rows.refs_2_, bf16[512,1024]{1,0:T(8,128)(2,1)S(1)} %get-tuple-element.45.b0, bf16[512,1024]{1,0:T(8,128)(2,1)S(1)} %get-tuple-element.46.b1, bf16[512,1024]{1,0:T(8,128)(2,1)S(1)} %get-tuple-element.47.b2, bf16[512,1024]{1,0:T(8,128)(2,1)S(1)} %get-tuple-element.48.b3), custom_call_target="tpu_custom_call" | custom-call | flops 1200000000 | bytes 131072 | tf_op jit(solution)/shard_map/piece/pallas_call | solution.py:94
  89.0 2.0 %piece.4 = f32[64,512]{1,0:T(8,128)S(1)} custom-call(f32[64,2048]{1,0:T(8,128)S(1)} %collective-permute-done.14.rows.refs_1_, bf16[512,1024]{1,0:T(8,128)(2,1)S(1)} %get-tuple-element.45.b0, bf16[512,1024]{1,0:T(8,128)(2,1)S(1)} %get-tuple-element.46.b1, bf16[512,1024]{1,0:T(8,128)(2,1)S(1)} %get-tuple-element.47.b2, bf16[512,1024]{1,0:T(8,128)(2,1)S(1)} %get-tuple-element.48.b3), custom_call_target="tpu_custom_call" | custom-call | flops 1200000000 | bytes 131072 | tf_op jit(solution)/shard_map/piece/pallas_call | solution.py:94
  95.5 2.4 %collective-permute-done.15 = f32[64,512]{1,0:T(8,128)S(1)} collective-permute-done((f32[64,512]{1,0:T(8,128)S(1)}, f32[64,512]{1,0:T(8,128)S(1)}, u32[]{:S(2)}, u32[]{:S(2)}) %collective-permute-start.15) | collective-permute-done | bytes 131104 | tf_op jit(solution)/shard_map/ppermute | solution.py:277
  102.5 2.2 %collective-permute-done.19.refs_11_ = f32[64,512]{1,0:T(8,128)S(1)} collective-permute-done((f32[64,512]{1,0:T(8,128)S(1)}, f32[64,512]{1,0:T(8,128)S(1)}, u32[]{:S(2)}, u32[]{:S(2)}) %collective-permute-start.19) | collective-permute-done | bytes 131104 | tf_op jit(solution)/shard_map/ppermute | solution.py:277
  106.1 1.5 %finish.1 = (f32[256,512]{1,0:T(8,128)}, f32[64,1024]{1,0:T(8,128)}) custom-call(s32[2]{0:T(128)S(1)} %pad_add_fusion.where, f32[256,512]{1,0:T(8,128)S(1)} %add.33.refs_0_, f32[256,512]{1,0:T(8,128)S(1)} %collective-permute-done.6.refs_1_, f32[256,512]{1,0:T(8,128)S(1)} %add.34.refs_2_, f32[256,512]{1,0:T(8,128)S(1)} %collective-permute-done.8.refs_3_, ...), custom_call_target="tpu_custom_call" | custom-call | bytes 786432 | tf_op jit(solution)/shard_map/finish/pallas_call | solution.py:94
  (48 shorter events, 23.4 us)
Async XLA Ops:
  0.6 5.5 %collective-permute-start = (f32[512,1024]{1,0:T(8,128)}, f32[512,1024]{1,0:T(8,128)S(1)}, u32[]{:S(2)}, u32[]{:S(2)}) collective-permute-start(f32[512,1024]{1,0:T(8,128)} %value.1), channel_id=1, source_target_pairs={{0,1},{1,0},{2,3},{3,2},{4,5},{5,4},{6,7},{7,6},{8,9},{9,8},{10,11... | collective-permute-start | bytes 6291464 | tf_op jit(solution)/shard_map/ppermute | solution.py:277
  2.0 15.0 %collective-permute-start.1 = (f32[256,1024]{1,0:T(8,128)S(1)}, f32[256,1024]{1,0:T(8,128)}, u32[]{:S(2)}, u32[]{:S(2)}) collective-permute-start(f32[256,1024]{1,0:T(8,128)S(1)} %dynamic-slice_bitcast_fusion.1.near), channel_id=1, source_target_pairs={{16,0},{9,1},{18,2},{11,3},{20,4},{13,5},{22,6},{15,7},{0,8},{25,9... | collective-permute-start | bytes 3145736 | tf_op jit(solution)/shard_map/ppermute | solution.py:277
  4.3 1.0 copy-start.1
  6.2 1.7 %copy-start = (f32[512,1024]{1,0:T(8,128)S(1)}, f32[512,1024]{1,0:T(8,128)}, u32[]{:S(2)}) copy-start(f32[512,1024]{1,0:T(8,128)} %value.1) | copy-start | bytes 6291460
  6.3 23.2 %collective-permute-start.3 = (f32[288,1024]{1,0:T(8,128)S(1)}, f32[288,1024]{1,0:T(8,128)S(1)}, u32[]{:S(2)}, u32[]{:S(2)}) collective-permute-start(f32[288,1024]{1,0:T(8,128)S(1)} %pad_maximum_fusion), channel_id=1, source_target_pairs={{16,0},{9,1},{18,2},{11,3},{20,4},{13,5},{22,6},{15,7},{0,8},{25,9... | collective-permute-start | bytes 3538952 | tf_op jit(solution)/shard_map/ppermute | solution.py:277
  17.0 23.8 %collective-permute-start.2 = (f32[256,1024]{1,0:T(8,128)}, f32[256,1024]{1,0:T(8,128)S(1)}, u32[]{:S(2)}, u32[]{:S(2)}) collective-permute-start(f32[256,1024]{1,0:T(8,128)} %collective-permute-done.1.near), channel_id=1, source_target_pairs={{16,0},{9,1},{18,2},{11,3},{20,4},{13,5},{22,6},{15,7},{0,8},{25,9... | collective-permute-start | bytes 3145736 | tf_op jit(solution)/shard_map/ppermute | solution.py:277
  18.5 13.1 %collective-permute-start.4 = (f32[256,512]{1,0:T(8,128)S(1)}, f32[256,512]{1,0:T(8,128)S(1)}, u32[]{:S(2)}, u32[]{:S(2)}) collective-permute-start(f32[256,512]{1,0:T(8,128)S(1)} %get-tuple-element.58), channel_id=1, source_target_pairs={{2,0},{6,4},{3,1},{7,5},{8,10},{14,12},{9,11},{15,13},{16,18},{22,... | collective-permute-start | bytes 1572872 | tf_op jit(solution)/shard_map/ppermute | solution.py:277
  29.5 34.2 %collective-permute-start.5 = (f32[288,1024]{1,0:T(8,128)S(1)}, f32[288,1024]{1,0:T(8,128)S(1)}, u32[]{:S(2)}, u32[]{:S(2)}) collective-permute-start(f32[288,1024]{1,0:T(8,128)S(1)} %collective-permute-done.3.far), channel_id=1, source_target_pairs={{16,0},{9,1},{18,2},{11,3},{20,4},{13,5},{22,6},{15,7},{0,8},{25,9... | collective-permute-start | bytes 3538952 | tf_op jit(solution)/shard_map/ppermute | solution.py:277
  40.8 25.4 %collective-permute-start.9 = (f32[136,2048]{1,0:T(8,128)S(1)}, f32[136,2048]{1,0:T(8,128)S(1)}, u32[]{:S(2)}, u32[]{:S(2)}) collective-permute-start(f32[136,2048]{1,0:T(8,128)S(1)} %get-tuple-element.66), channel_id=1, source_target_pairs={{8,0},{17,1},{10,2},{19,3},{12,4},{21,5},{14,6},{23,7},{24,8},{1,9... | collective-permute-start | bytes 3342344 | tf_op jit(solution)/shard_map/ppermute | solution.py:277
  42.3 15.0 %collective-permute-start.7 = (f32[256,512]{1,0:T(8,128)S(1)}, f32[256,512]{1,0:T(8,128)S(1)}, u32[]{:S(2)}, u32[]{:S(2)}) collective-permute-start(f32[256,512]{1,0:T(8,128)S(1)} %get-tuple-element.62), channel_id=1, source_target_pairs={{0,2},{6,4},{1,3},{7,5},{10,8},{14,12},{9,11},{13,15},{16,18},{20,... | collective-permute-start | bytes 1572872 | tf_op jit(solution)/shard_map/ppermute | solution.py:277
  43.6 13.8 %collective-permute-start.6 = (f32[256,512]{1,0:T(8,128)S(1)}, f32[256,512]{1,0:T(8,128)S(1)}, u32[]{:S(2)}, u32[]{:S(2)}) collective-permute-start(f32[256,512]{1,0:T(8,128)S(1)} %add.33.refs_0_), channel_id=1, source_target_pairs={{4,0},{5,1},{12,10},{13,11},{18,20},{19,21},{26,30},{27,31}} | collective-permute-start | bytes 1572872 | tf_op jit(solution)/shard_map/ppermute | solution.py:277
  66.2 16.8 %collective-permute-start.10 = (f32[256,512]{1,0:T(8,128)S(1)}, f32[256,512]{1,0:T(8,128)S(1)}, u32[]{:S(2)}, u32[]{:S(2)}) collective-permute-start(f32[256,512]{1,0:T(8,128)S(1)} %get-tuple-element.72), channel_id=1, source_target_pairs={{0,2},{4,6},{1,3},{5,7},{8,10},{14,12},{9,11},{15,13},{16,18},{22,... | collective-permute-start | bytes 1572872 | tf_op jit(solution)/shard_map/ppermute | solution.py:277
  67.5 18.0 %collective-permute-start.17 = (f32[64,2048]{1,0:T(8,128)S(1)}, f32[64,2048]{1,0:T(8,128)S(1)}, u32[]{:S(2)}, u32[]{:S(2)}) collective-permute-start(f32[64,2048]{1,0:T(8,128)S(1)} %get-tuple-element.75), channel_id=1, source_target_pairs={{8,0},{17,1},{10,2},{19,3},{12,4},{21,5},{14,6},{23,7},{24,8},{1,9... | collective-permute-start | bytes 1572872 | tf_op jit(solution)/shard_map/ppermute | solution.py:277
  69.0 20.0 %collective-permute-start.14 = (f32[64,2048]{1,0:T(8,128)S(1)}, f32[64,2048]{1,0:T(8,128)S(1)}, u32[]{:S(2)}, u32[]{:S(2)}) collective-permute-start(f32[64,2048]{1,0:T(8,128)S(1)} %get-tuple-element.74), channel_id=1, source_target_pairs={{8,0},{17,1},{10,2},{19,3},{12,4},{21,5},{14,6},{23,7},{24,8},{1,9... | collective-permute-start | bytes 1572872 | tf_op jit(solution)/shard_map/ppermute | solution.py:277
  71.6 27.6 %collective-permute-start.8 = (f32[256,512]{1,0:T(8,128)S(1)}, f32[256,512]{1,0:T(8,128)S(1)}, u32[]{:S(2)}, u32[]{:S(2)}) collective-permute-start(f32[256,512]{1,0:T(8,128)S(1)} %add.34.refs_2_), channel_id=1, source_target_pairs={{2,4},{5,3},{12,8},{11,15},{18,22},{21,17},{28,26},{27,29}} | collective-permute-start | bytes 1572872 | tf_op jit(solution)/shard_map/ppermute | solution.py:277
  76.2 16.1 %collective-permute-start.12 = (f32[128,512]{1,0:T(8,128)S(1)}, f32[128,512]{1,0:T(8,128)S(1)}, u32[]{:S(2)}, u32[]{:S(2)}) collective-permute-start(f32[128,512]{1,0:T(8,128)S(1)} %piece.3), channel_id=1, source_target_pairs={{0,2},{6,4},{1,3},{7,5},{8,10},{12,14},{11,9},{15,13},{18,16},{22,... | collective-permute-start | bytes 786440 | tf_op jit(solution)/shard_map/ppermute | solution.py:277
  83.0 23.1 %collective-permute-start.11 = (f32[256,512]{1,0:T(8,128)S(1)}, f32[256,512]{1,0:T(8,128)S(1)}, u32[]{:S(2)}, u32[]{:S(2)}) collective-permute-start(f32[256,512]{1,0:T(8,128)S(1)} %add.35.refs_4_), channel_id=1, source_target_pairs={{2,6},{3,7},{10,12},{11,13},{20,18},{21,19},{28,24},{29,25}} | collective-permute-start | bytes 1572872 | tf_op jit(solution)/shard_map/ppermute | solution.py:277
  87.5 7.9 %collective-permute-start.18 = (f32[64,512]{1,0:T(8,128)S(1)}, f32[64,512]{1,0:T(8,128)S(1)}, u32[]{:S(2)}, u32[]{:S(2)}) collective-permute-start(f32[64,512]{1,0:T(8,128)S(1)} %piece.5), channel_id=1, source_target_pairs={{0,2},{6,4},{1,3},{7,5},{8,10},{12,14},{11,9},{15,13},{18,16},{22,... | collective-permute-start | bytes 393224 | tf_op jit(solution)/shard_map/ppermute | solution.py:277
  91.0 6.9 %collective-permute-start.15 = (f32[64,512]{1,0:T(8,128)S(1)}, f32[64,512]{1,0:T(8,128)S(1)}, u32[]{:S(2)}, u32[]{:S(2)}) collective-permute-start(f32[64,512]{1,0:T(8,128)S(1)} %piece.4), channel_id=1, source_target_pairs={{0,2},{6,4},{1,3},{7,5},{8,10},{12,14},{11,9},{15,13},{18,16},{22,... | collective-permute-start | bytes 393224 | tf_op jit(solution)/shard_map/ppermute | solution.py:277
  92.4 10.1 %collective-permute-start.13 = (f32[128,512]{1,0:T(8,128)S(1)}, f32[128,512]{1,0:T(8,128)S(1)}, u32[]{:S(2)}, u32[]{:S(2)}) collective-permute-start(f32[128,512]{1,0:T(8,128)S(1)} %add.36.refs_6_), channel_id=1, source_target_pairs={{4,2},{3,5},{10,14},{13,9},{20,16},{19,23},{26,28},{29,27}} | collective-permute-start | bytes 786440 | tf_op jit(solution)/shard_map/ppermute | solution.py:277
  95.4 7.1 %collective-permute-start.20 = (f32[64,1024]{1,0:T(8,128)S(1)}, f32[64,1024]{1,0:T(8,128)S(1)}, u32[]{:S(2)}, u32[]{:S(2)}) collective-permute-start(f32[64,1024]{1,0:T(8,128)S(1)} %get-tuple-element.79), channel_id=1, source_target_pairs={{0,1},{1,0},{2,3},{3,2},{4,5},{5,4},{6,7},{7,6},{8,9},{9,8},{10,11... | collective-permute-start | bytes 786440 | tf_op jit(solution)/shard_map/ppermute | solution.py:277
  97.9 6.8 %collective-permute-start.19 = (f32[64,512]{1,0:T(8,128)S(1)}, f32[64,512]{1,0:T(8,128)S(1)}, u32[]{:S(2)}, u32[]{:S(2)}) collective-permute-start(f32[64,512]{1,0:T(8,128)S(1)} %add.38.refs_10_), channel_id=1, source_target_pairs={{4,2},{3,5},{10,14},{13,9},{20,16},{19,23},{26,28},{29,27}} | collective-permute-start | bytes 393224 | tf_op jit(solution)/shard_map/ppermute | solution.py:277
  99.2 6.9 %collective-permute-start.16 = (f32[64,512]{1,0:T(8,128)S(1)}, f32[64,512]{1,0:T(8,128)S(1)}, u32[]{:S(2)}, u32[]{:S(2)}) collective-permute-start(f32[64,512]{1,0:T(8,128)S(1)} %add.37.refs_8_), channel_id=1, source_target_pairs={{4,2},{3,5},{10,14},{13,9},{20,16},{19,23},{26,28},{29,27}} | collective-permute-start | bytes 393224 | tf_op jit(solution)/shard_map/ppermute | solution.py:277

commit v3 on v0

v3 whole, which is shorter than its diff:
```python
import functools

import jax
import jax.numpy as jnp
import numpy as np
from jax import lax
from jax.experimental import pallas as pl
from jax.experimental.pallas import tpu as pltpu
from jax.sharding import PartitionSpec as P

AXES = ("row", "col")
CORES = 2
CUTS = (0, 1, 2, 4, 6, 8)
BACK = (4, 4, 6)
PARAMS = pltpu.CompilerParams(vmem_limit_bytes=40 * 2**20)


def shape(*dims, dtype=jnp.float32):
    return jax.ShapeDtypeStruct(dims, dtype)


class Layout:
    def __init__(self, rows, cols):
        self.rows, self.cols, self.chips = rows, cols, cols // CORES
        self.subs = self.chips // rows
        self.rounds = self.chips.bit_length() - 1
        assert rows % 2 == 0 and rows >= 4 and self.chips == 1 << self.rounds and self.subs * rows == self.chips
        self.ring = [*range(0, rows, 2), *reversed(range(1, rows, 2))]
        self.place = {r: i for i, r in enumerate(self.ring)}
        self.devices = [(r, z, c) for r in range(rows) for z in range(self.chips) for c in range(CORES)]

    def flat(self, r, z, c):
        return r * self.cols + z * CORES + c

    def along(self, r, c, steps):
        return self.ring[(self.place[r] + (steps if c == 0 else -steps)) % self.rows]

    def swap(self):
        return [(self.flat(r, z, c), self.flat(r, z, 1 - c)) for r, z, c in self.devices]

    def fetch(self, steps):
        return [(self.flat(self.along(r, c, steps), z, c), self.flat(r, z, c)) for r, z, c in self.devices]

    def exchange(self, bit):
        return [(self.flat(r, z, c), self.flat(r, z ^ (1 << bit), c)) for r, z, c in self.devices]

    def slot(self, target, z):
        return int(format(target ^ z, f"0{self.rounds}b")[::-1], 2)

    def table(self):
        table = np.zeros((self.rows, self.cols, 1 + self.rows + self.chips), np.int32)
        for r, z, c in self.devices:
            takers = [self.along(r, c, -s) for s in range(self.rows)]
            slots = [self.slot(self.along(r, c, s) * self.subs + p, z) for s in range(self.rows) for p in range(self.subs)]
            table[r, z * CORES + c] = [c, *takers, *slots]
        return table


def halves(value):
    high = value.astype(jnp.bfloat16)
    return high, (value - high.astype(jnp.float32)).astype(jnp.bfloat16)


def product(left, right, dims):
    def one(a, b):
        return lax.dot_general(a, b, (dims, ((), ())), preferred_element_type=jnp.float32)

    return one(left[0], right[0]) + (one(left[0], right[1]) + one(left[1], right[0]))


def call(kernel, outs, *args, name, flops=0, smem=0, scratch=()):
    vmem = pl.BlockSpec(memory_space=pltpu.VMEM)
    specs = [pl.BlockSpec(memory_space=pltpu.SMEM)] * smem + [vmem] * (len(args) - smem)
    return pl.pallas_call(
        kernel,
        out_shape=outs,
        in_specs=specs,
        out_specs=[vmem] * len(outs),
        scratch_shapes=list(scratch),
        compiler_params=PARAMS,
        cost_estimate=pl.CostEstimate(flops=flops, bytes_accessed=4 * sum(o.size for o in outs), transcendentals=0),
        name=name,
    )(*args)


def call(kernel, outs, *args, name, flops=0, smem=0, scratch=()):
    vmem = pl.BlockSpec(memory_space=pltpu.VMEM)
    specs = [pl.BlockSpec(memory_space=pltpu.SMEM)] * smem + [vmem] * (len(args) - smem)
    return pl.pallas_call(
        kernel,
        out_shape=outs,
        in_specs=specs,
        out_specs=[vmem] * len(outs),
        scratch_shapes=list(scratch),
        compiler_params=PARAMS,
        cost_estimate=pl.CostEstimate(flops=flops, bytes_accessed=4 * sum(o.size for o in outs), transcendentals=0),
        name=name,
    )(*args)


class Extra:
    def __init__(self, count, rank, half, width):
        self.count, self.rank, self.half, self.width = count, rank, half, width
        self.folds = 1
        while 2 * self.folds * count * half <= width and rank % (16 * self.folds) == 0:
            self.folds *= 2
        self.height = rank // self.folds

    def lanes(self, fold, index):
        first = (fold * self.count + index) * self.half
        return slice(first, first + self.half)

    def write(self, out, index, matrix):
        for f in range(self.folds):
            out[:, self.lanes(f, index)] = matrix[f * self.height : (f + 1) * self.height]

    def read(self, rows, index):
        return jnp.concatenate([rows[:, self.lanes(f, index)] for f in range(self.folds)], axis=0)


def weights_kernel(subs, ahead, behind, where, factor, own, out_ahead, out_behind, turned):
    rank = ahead.rank
    part = factor.shape[0] // (subs * CORES)
    size = part // 2
    for n in range(CORES):
        core = (where[0] + n) % CORES
        rows = [
            factor[pl.ds(pl.multiple_of((s * CORES + core) * part + g * size, size), size), :]
            for g in range(2)
            for s in range(subs)
        ]
        turned[n] = jnp.concatenate(rows, axis=0).T

    def columns(steps, n=0):
        return turned[n, pl.ds(pl.multiple_of(where[1 + steps] * rank, rank), rank), :]

    for n in range(CORES):
        own[n] = columns(0, n)
    for i in range(ahead.count):
        ahead.write(out_ahead, i, columns(1 + i))
    for i in range(behind.count):
        behind.write(out_behind, i, columns(ahead.count + behind.count - i))


def prepare_kernel(subs, cuts, tensor, ride_ahead, ride_behind, high, low, *outs):
    high[...], low[...] = halves(tensor[...])
    part = tensor.shape[0] // (subs * CORES)
    for a, b, out in zip([cuts[0], *cuts], [cuts[1], *cuts[1:]], outs):
        size = b - a
        for c in range(CORES):
            for s in range(subs):
                first, to = (s * CORES + c) * part + a, (c * subs + s) * size
                out[to : to + size, :] = tensor[first : first + size, :]
    rows = CORES * subs * (cuts[1] - cuts[0])
    outs[0][rows:, :] = ride_ahead[...]
    outs[1][rows:, :] = ride_behind[...]


def gram_kernel(subs, where, *refs):
    *chunks, high, low, keep, send = refs
    size = keep.shape[1]
    rows = CORES * subs * size
    left = halves(jnp.concatenate([c[:rows, :] for c in chunks], axis=0))
    total = product(left, (high[...], low[...]), ((1,), (1,)))
    for k in range(len(chunks)):
        for c in range(CORES):
            for s in range(subs):
                slot = where[1 + len(chunks) + k * subs + s]
                first = ((k * CORES + c) * subs + s) * size

                @pl.when(where[0] == c)
                def _(slot=slot, first=first):
                    keep[slot] = total[first : first + size]

                @pl.when(where[0] != c)
                def _(slot=slot, first=first):
                    send[slot] = total[first : first + size]


def fold_kernel(keep, received, new_keep, new_send):
    slots = new_keep.shape[0]
    new_keep[...] = keep[:slots] + received[:slots]
    new_send[...] = keep[slots:] + received[slots:]


def core_kernel(subs, group, sizes, extras, where, *refs):
    *refs, out = refs
    refs = list(refs)
    own = refs.pop(0)
    mine = [refs.pop(0) for _ in extras]
    other = refs.pop(0)
    half = own.shape[2] // 2
    lanes = slice(group * half, (group + 1) * half)
    weights = [(own[0][:, lanes], own[1][:, lanes])]
    for rows, (extra, index, (extra2, index2, first)) in zip(mine, extras):
        near = extra.read(rows[rows.shape[0] - extra.height :, :], index)
        far = extra2.read(other[first : first + extra2.height, :], index2)
        weights.append((near[:, lanes], far[:, lanes]))
    first = where[0] == 0
    sides = [jnp.where(first, w[n], w[1 - n]) for w in weights for n in range(CORES)]
    weights = halves(jnp.concatenate(sides, axis=1))
    count = len(sizes)
    whole = []
    for k in range(len(extras) + 1):
        chunks = refs[k * count : (k + 1) * count]
        for c in range(CORES):
            for s in range(subs):
                for chunk, size in zip(chunks, sizes):
                    at = (c * subs + s) * size
                    whole.append(chunk[at : at + size, :])
    share = product(weights, halves(jnp.concatenate(whole, axis=0)), ((1,), (0,)))
    before = refs[(len(extras) + 1) * count :]
    out[...] = before[0][...] + share if before else share


def finish_kernel(cuts, inverse, *refs):
    *refs, gram = refs
    for n, (a, b) in enumerate(zip(cuts, cuts[1:])):
        gram[a:b, :] = (refs[2 * n][0] + refs[2 * n + 1][0]) * inverse


def body(tensor, factor):
    layout = Layout(lax.axis_size("row"), lax.axis_size("col"))
    rows, subs, chips = layout.rows, layout.subs, layout.chips
    block, width = tensor.shape
    inverse = 1.0 / (width * layout.cols)
    row, col = lax.axis_index("row"), lax.axis_index("col")
    core = lax.rem(col, CORES)
    part = block // (subs * CORES)
    rank = factor.shape[1] // rows
    cuts = [part * n // 8 for n in CUTS]
    sizes = [b - a for a, b in zip(cuts, cuts[1:])]
    chunks = range(len(sizes))
    bf16 = jnp.bfloat16

    def send(value, pairs):
        return lax.ppermute(value, AXES, pairs)

    arrived = []

    def fetch(value, steps, work=(), back=BACK[0]):
        names = [(arrived, len(arrived) - back)] if len(arrived) >= back else []
        names += work
        if names:
            value, *held = lax.optimization_barrier((value, *(a[i] for a, i in names)))
            for (a, i), h in zip(names, held):
                a[i] = h
        arrived.append(send(value, layout.fetch(steps)))
        return len(arrived) - 1

    size = sizes[0]
    split_rows = tensor.reshape(subs, CORES, part, width).swapaxes(0, 1)
    own = {(0, w): split_rows[:, :, :size].reshape(CORES * subs * size, width) for w in (1, -1)}
    at = {(0, s): fetch(own[0, w], w) for s, w in ((1, 1), (rows - 1, -1))}

    table = jnp.asarray(layout.table())
    where = lax.dynamic_slice(table, (row, col, 0), (1, 1, table.shape[2])).reshape(-1)
    half = subs * part
    last = rows // 2
    ahead, behind = Extra(last, rank, half, width), Extra(rows - 1 - last, rank, half, width)
    own_weights, ride_ahead, ride_behind = call(
        functools.partial(weights_kernel, subs, ahead, behind),
        [shape(CORES, rank, half), shape(ahead.height, width), shape(behind.height, width)],
        where,
        factor,
        name="weights",
        smem=1,
        scratch=[pltpu.VMEM((CORES, factor.shape[1], half), jnp.float32)],
    )
    heights = [CORES * subs * n for n in (sizes[1], *sizes[1:])]
    heights[0] += ahead.height
    heights[1] += behind.height
    ready = call(
        functools.partial(prepare_kernel, subs, cuts[1:]),
        [shape(block, width, dtype=bf16)] * 2 + [shape(n, width) for n in heights],
        tensor,
        ride_ahead,
        ride_behind,
        name="prepare",
    )
    pair = list(ready[:2])
    own.update({(n, w): p for n, p in enumerate(ready[4:], 2) for w in (1, -1)})
    own[1, 1], own[1, -1] = ready[2:4]

    order = [1, *(s for i in range(1, last) for s in (rows - i, i + 1))]

    def got(chunk, steps, way=1):
        return own[chunk, way] if steps == 0 else arrived[at[chunk, steps]]

    def gather(chunk, steps, work, back):
        way = 1 if steps <= last else -1
        value = got(chunk, steps - 1 if steps <= last else (steps + 1) % rows, way)
        at[chunk, steps] = fetch(value, way, work, back)

    def grams(chunk):
        size = sizes[chunk]
        return call(
            functools.partial(gram_kernel, subs),
            [shape(chips, size, block)] * 2,
            where,
            *(got(chunk, s) for s in range(rows)),
            *pair,
            name="gram",
            flops=12 * rows * subs * size * block * width,
            smem=1,
        )

    exchanges = [layout.swap(), *(layout.exchange(bit) for bit in range(layout.rounds))]

    def fold(state, n):
        keep, out = state
        received = send(out, exchanges[n])
        if n + 1 == len(exchanges):
            return [keep, received]
        return call(fold_kernel, [shape(keep.shape[0] // 2, *keep.shape[1:])] * 2, keep, received, name="fold")

    ride = [(ahead, s - 1) if s <= last else (behind, rows - 1 - s) for s in range(1, rows)]

    def swap_weights():
        held = [got(1, s) for s in range(1, rows)]
        return send(jnp.concatenate([v[v.shape[0] - e.height :] for v, (e, _) in zip(held, ride)], axis=0), layout.swap())

    def core_share(group, shares):
        parts = [n for n in chunks if cuts[n] * 2 // part == group]
        firsts = np.cumsum([0, *(e.height for e, _ in ride)])
        extras = [(*ride[s - 1], (*ride[rows - s - 1], int(firsts[rows - s - 1]))) for s in range(1, rows)]
        return call(
            functools.partial(core_kernel, subs, group, [sizes[n] for n in parts], extras),
            [shape(rank, width)],
            where,
            own_weights,
            *(got(1, s) for s in range(1, rows)),
            other_weights,
            *(got(n, s) for s in range(rows) for n in parts),
            *shares,
            name="core",
            flops=6 * rank * half * rows * width,
            smem=1,
        )

    states, rounds = {}, {}

    def advance(n):
        if n in states and rounds[n] < len(exchanges):
            states[n] = list(fold(states[n], rounds[n]))
            rounds[n] += 1

    def held(n):
        return [(states[n], 0), (states[n], 1)] if n in states else []

    def plan():
        for n in chunks:
            for i, steps in enumerate(order):
                if i == len(order) - 1 and n + 1 < len(sizes):
                    yield n + 1, 0, order[0]
                if i > 0 or n == 0:
                    yield n, i, steps

    for n, i, steps in plan():
        final = i == len(order) - 1
        if (n, steps) not in at:
            gather(n, steps, [(pair, 0)] if n == 0 else [], BACK[2] if final else BACK[min(i, 1)])
        if not final:
            continue
        for back, count in ((1, 2), (2, len(exchanges))):
            while n - back in rounds and rounds[n - back] < count:
                advance(n - back)
        names = [t for back in (1, 2, 3) for t in held(n - back)]
        if names:
            own[n, 1], *values = lax.optimization_barrier((own[n, 1], *(a[i] for a, i in names)))
            for (a, i), value in zip(names, values):
                a[i] = value
        states[n], rounds[n] = list(grams(n)), 0
    other_weights = swap_weights()
    share = core_share(0, [])
    while any(rounds[i] < len(exchanges) for i in chunks):
        for i in chunks:
            if i == n and rounds[n] == 2:
                states[n][0], states[n - 1][1] = lax.optimization_barrier((states[n][0], states[n - 1][1]))
            advance(i)
        if rounds[n] == 2:
            own_weights, states[n][0] = lax.optimization_barrier((own_weights, states[n][0]))
    done = [a for n in chunks for a in states[n]]

    (core_rows,) = core_share(1, share)
    (gram,) = call(functools.partial(finish_kernel, cuts, inverse), [shape(part, block)], *done, name="finish")
    return (gram, core_rows)


def solution(mesh):
    placed = (P("row", "col"), P("row", None))
    return jax.shard_map(
        body,
        mesh=mesh,
        in_specs=placed,
        out_specs=(P("col", "row"), P("row", "col")),
        check_vma=False,
    )
```

time: 191 us -> 108 us (0.57)
  waiting for transfers between devices: 155 us -> 44.3 us
  starting transfers between devices: 0.12 us -> 39.7 us
  matrix products: 21.4 us -> 0 us
  Pallas kernels: 0 us -> 18.3 us
  between operations: 13.8 us -> 0.87 us
  local copies, waits for them, and re-layouts: 0.25 us -> 4.32 us
    all_gather x1 -> x0, waiting for transfers between devices: 87.4 us -> none  [body(): gathered = lax.all_gather(tensor, 'row', axis=0, tiled=True)]
    reduce_scatter x2 -> x0, waiting for transfers between devices: 67.3 us -> none  [the longest x1 53 us: body(): lax.psum_scatter(product(gathered, tensor) * inverse, 'col', scatter_dime...]
    ppermute x0 -> x31, waiting for transfers between devices: none -> 44.3 us  [send(): return lax.ppermute(value, AXES, pairs)]
    ppermute x0 -> x31, starting transfers between devices: none -> 39.7 us  [send(): return lax.ppermute(value, AXES, pairs)]
    dot_general x2 -> x0, matrix products: 21.4 us -> none  [the longest x1 16.9 us: product(): lax.dot_general(left, right_rows, (((1,), (1,)), ((), ())), precision=lax...]
    pallas_call x0 -> x20, Pallas kernels: none -> 18.3 us  [call(): pl.pallas_call(kernel, out_shape=outs, in_specs=specs, out_specs=[vmem] *...]
    unnamed x4, local copies, waits for them, and re-layouts: 0.25 us -> 2.63 us
  transfers between devices with their start and end apart: 3 -> 31, of which waited for: 3 -> 13; matrix products, arithmetic and copies ran while one was open for 11% -> 1% of each run, Pallas kernels for 0% -> 14%
where the time goes in v3:
time: 108 us
  waiting for transfers between devices  44.3 us (41%)
  starting transfers between devices  39.7 us (37%)
  Pallas kernels  18.3 us (17%)
  local copies, waits for them, and re-layouts  4.32 us (4%)
    ppermute x31, waiting for transfers between devices, send(): return lax.ppermute(value, AXES, pairs)  44.3 us
    ppermute x31, starting transfers between devices, send(): return lax.ppermute(value, AXES, pairs)  39.7 us
    pallas_call x20, Pallas kernels, call(): pl.pallas_call(kernel, out_shape=outs, in_specs=specs, out_specs=[vmem] *...  18.3 us
    unnamed x4, local copies, waits for them, and re-layouts  2.63 us
  transfers between devices with their start and end apart: 31, of which 13 were waited for; matrix products, arithmetic and copies ran while one was open for 1% of the time, Pallas kernels for 14%

profile of v3, /device:TPU:0, one launch (start us, length us, event | category | flops | bytes accessed | tf_op | source)
XLA Modules:
  0.0 107.6 jit_solution(5967214388368123236)
XLA Ops:
  1.6 3.0 %collective-permute-start = (f32[64,1024]{1,0:T(8,128)S(1)}, f32[64,1024]{1,0:T(8,128)S(1)}, u32[]{:S(2)}, u32[]{:S(2)}) collective-permute-start(f32[64,1024]{1,0:T(8,128)S(1)} %bitcast.5), channel_id=1, source_target_pairs={{16,0},{9,1},{18,2},{11,3},{20,4},{13,5},{22,6},{15,7},{0,8},{25,9... | collective-permute-start | bytes 786440 | tf_op jit(solution)/shard_map/ppermute | solution.py:237
  9.2 2.0 %collective-permute-start.5 = (f32[96,1024]{1,0:T(8,128)S(1)}, f32[96,1024]{1,0:T(8,128)S(1)}, u32[]{:S(2)}, u32[]{:S(2)}) collective-permute-start(f32[96,1024]{1,0:T(8,128)S(1)} %get-tuple-element.107.refs_0_.refs_6_), channel_id=1, source_target_pairs={{16,0},{9,1},{18,2},{11,3},{20,4},{13,5},{22,6},{15,7},{0,8},{25,9... | collective-permute-start | bytes 1179656 | tf_op jit(solution)/shard_map/ppermute | solution.py:237
  14.4 5.5 %collective-permute-done.1.refs_2_.refs_11_ = f32[64,1024]{1,0:T(8,128)S(1)} collective-permute-done((f32[64,1024]{1,0:T(8,128)S(1)}, f32[64,1024]{1,0:T(8,128)S(1)}, u32[]{:S(2)}, u32[]{:S(2)}) %collective-permute-start.1) | collective-permute-done | bytes 262176 | tf_op jit(solution)/shard_map/ppermute | solution.py:237
  19.9 1.7 %gram.5 = (f32[4,32,512]{2,1,0:T(8,128)S(1)}, f32[4,32,512]{2,1,0:T(8,128)S(1)}) custom-call(s32[9]{0:T(128)S(1)} %dynamic-slice_bitcast_fusion.where, f32[64,1024]{1,0:T(8,128)S(1)} %bitcast.7, f32[64,1024]{1,0:T(8,128)S(1)} %collective-permute-done.refs_1_.refs_8_, f32[64,1024]{1,0:T(8,128)S(1)} %collective-permute-done.1.refs_2_.refs_11_, ...), custom_call_target="tpu_custom_call" | custom-call | flops 805306368 | bytes 524288 | tf_op jit(solution)/shard_map/gram/pallas_call | solution.py:89
  21.7 2.0 %collective-permute-start.6 = (f32[96,1024]{1,0:T(8,128)S(1)}, f32[96,1024]{1,0:T(8,128)S(1)}, u32[]{:S(2)}, u32[]{:S(2)}) collective-permute-start(f32[96,1024]{1,0:T(8,128)S(1)} %collective-permute-done.5.refs_1_.refs_9_), channel_id=1, source_target_pairs={{16,0},{9,1},{18,2},{11,3},{20,4},{13,5},{22,6},{15,7},{0,8},{25,9... | collective-permute-start | bytes 1179656 | tf_op jit(solution)/shard_map/ppermute | solution.py:237
  23.8 2.1 %collective-permute-start.4 = (f32[2,32,512]{2,1,0:T(8,128)S(1)}, f32[2,32,512]{2,1,0:T(8,128)S(1)}, u32[]{:S(2)}, u32[]{:S(2)}) collective-permute-start(f32[2,32,512]{2,1,0:T(8,128)S(1)} %get-tuple-element.104), channel_id=1, source_target_pairs={{0,2},{1,3},{2,0},{3,1},{4,6},{5,7},{6,4},{7,5},{8,10},{9,11},{10,... | collective-permute-start | bytes 393224 | tf_op jit(solution)/shard_map/ppermute | solution.py:237
  29.4 4.9 %collective-permute-done.7.refs_3_.refs_15_ = f32[80,1024]{1,0:T(8,128)S(1)} collective-permute-done((f32[80,1024]{1,0:T(8,128)S(1)}, f32[80,1024]{1,0:T(8,128)S(1)}, u32[]{:S(2)}, u32[]{:S(2)}) %collective-permute-start.7) | collective-permute-done | bytes 327712 | tf_op jit(solution)/shard_map/ppermute | solution.py:237
  39.3 1.9 %collective-permute-start.17 = (f32[128,1024]{1,0:T(8,128)S(1)}, f32[128,1024]{1,0:T(8,128)S(1)}, u32[]{:S(2)}, u32[]{:S(2)}) collective-permute-start(f32[128,1024]{1,0:T(8,128)S(1)} %get-tuple-element.142.refs_0_.refs_5_), channel_id=1, source_target_pairs={{16,0},{9,1},{18,2},{11,3},{20,4},{13,5},{22,6},{15,7},{0,8},{25,9... | collective-permute-start | bytes 1572872 | tf_op jit(solution)/shard_map/ppermute | solution.py:237
  41.2 2.6 %collective-permute-start.10 = (f32[1,32,512]{2,1,0:T(8,128)S(1)}, f32[1,32,512]{2,1,0:T(8,128)S(1)}, u32[]{:S(2)}, u32[]{:S(2)}) collective-permute-start(f32[1,32,512]{2,1,0:T(8,128)S(1)} %get-tuple-element.119), channel_id=1, source_target_pairs={{0,4},{1,5},{2,6},{3,7},{4,0},{5,1},{6,2},{7,3},{8,12},{9,13},{10,... | collective-permute-start | bytes 196616 | tf_op jit(solution)/shard_map/ppermute | solution.py:237
  43.8 3.3 %collective-permute-done.10.refs_1_ = f32[1,32,512]{2,1,0:T(8,128)S(1)} collective-permute-done((f32[1,32,512]{2,1,0:T(8,128)S(1)}, f32[1,32,512]{2,1,0:T(8,128)S(1)}, u32[]{:S(2)}, u32[]{:S(2)}) %collective-permute-start.10) | collective-permute-done | bytes 65568 | tf_op jit(solution)/shard_map/ppermute | solution.py:237
  47.2 2.5 %gram.7 = (f32[4,64,512]{2,1,0:T(8,128)S(1)}, f32[4,64,512]{2,1,0:T(8,128)S(1)}) custom-call(s32[9]{0:T(128)S(1)} %dynamic-slice_bitcast_fusion.where, f32[128,1024]{1,0:T(8,128)S(1)} %get-tuple-element.124.refs_0_.refs_7_, f32[128,1024]{1,0:T(8,128)S(1)} %collective-permute-done.11.refs_1_.refs_10_, ...), custom_call_target="tpu_custom_call" | custom-call | flops 1610612736 | bytes 1048576 | tf_op jit(solution)/shard_map/gram/pallas_call | solution.py:89
  55.2 2.6 %collective-permute-start.16 = (f32[1,32,512]{2,1,0:T(8,128)S(1)}, f32[1,32,512]{2,1,0:T(8,128)S(1)}, u32[]{:S(2)}, u32[]{:S(2)}) collective-permute-start(f32[1,32,512]{2,1,0:T(8,128)S(1)} %get-tuple-element.132), channel_id=1, source_target_pairs={{0,4},{1,5},{2,6},{3,7},{4,0},{5,1},{6,2},{7,3},{8,12},{9,13},{10,... | collective-permute-start | bytes 196616 | tf_op jit(solution)/shard_map/ppermute | solution.py:237
  57.8 3.8 %collective-permute-done.15.received = f32[2,64,512]{2,1,0:T(8,128)S(1)} collective-permute-done((f32[2,64,512]{2,1,0:T(8,128)S(1)}, f32[2,64,512]{2,1,0:T(8,128)S(1)}, u32[]{:S(2)}, u32[]{:S(2)}) %collective-permute-start.15) | collective-permute-done | bytes 262176 | tf_op jit(solution)/shard_map/ppermute | solution.py:237
  61.6 2.1 %collective-permute-done.19.refs_3_.refs_11_ = f32[128,1024]{1,0:T(8,128)S(1)} collective-permute-done((f32[128,1024]{1,0:T(8,128)S(1)}, f32[128,1024]{1,0:T(8,128)S(1)}, u32[]{:S(2)}, u32[]{:S(2)}) %collective-permute-start.19) | collective-permute-done | bytes 524320 | tf_op jit(solution)/shard_map/ppermute | solution.py:237
  64.1 2.5 %gram.8 = (f32[4,64,512]{2,1,0:T(8,128)S(1)}, f32[4,64,512]{2,1,0:T(8,128)S(1)}) custom-call(s32[9]{0:T(128)S(1)} %dynamic-slice_bitcast_fusion.where, f32[128,1024]{1,0:T(8,128)S(1)} %get-tuple-element.142.refs_0_.refs_5_, f32[128,1024]{1,0:T(8,128)S(1)} %collective-permute-done.17.refs_1_.refs_7_, f32[128,1024]{1,0:T(8,128)S(1)} %collective-permute-done.18.refs_2_.refs_9_, ...), custom_call_target="tpu_custom_call" | custom-call | flops 1610612736 | bytes 1048576 | tf_op jit(solution)/shard_map/gram/pallas_call | solution.py:89
  69.7 1.7 %collective-permute-start.24 = (f32[128,1024]{1,0:T(8,128)S(1)}, f32[128,1024]{1,0:T(8,128)S(1)}, u32[]{:S(2)}, u32[]{:S(2)}) collective-permute-start(f32[128,1024]{1,0:T(8,128)S(1)} %collective-permute-done.23.refs_1_.refs_8_), channel_id=1, source_target_pairs={{16,0},{9,1},{18,2},{11,3},{20,4},{13,5},{22,6},{15,7},{0,8},{25,9... | collective-permute-start | bytes 1572872 | tf_op jit(solution)/shard_map/ppermute | solution.py:237
  72.0 1.9 %collective-permute-start.22 = (f32[1,64,512]{2,1,0:T(8,128)S(1)}, f32[1,64,512]{2,1,0:T(8,128)S(1)}, u32[]{:S(2)}, u32[]{:S(2)}) collective-permute-start(f32[1,64,512]{2,1,0:T(8,128)S(1)} %get-tuple-element.150), channel_id=1, source_target_pairs={{0,4},{1,5},{2,6},{3,7},{4,0},{5,1},{6,2},{7,3},{8,12},{9,13},{10,... | collective-permute-start | bytes 393224 | tf_op jit(solution)/shard_map/ppermute | solution.py:237
  73.9 8.3 %collective-permute-done.21.received = f32[2,64,512]{2,1,0:T(8,128)S(1)} collective-permute-done((f32[2,64,512]{2,1,0:T(8,128)S(1)}, f32[2,64,512]{2,1,0:T(8,128)S(1)}, u32[]{:S(2)}, u32[]{:S(2)}) %collective-permute-start.21) | collective-permute-done | bytes 262176 | tf_op jit(solution)/shard_map/ppermute | solution.py:237
  82.2 2.7 %gram.9 = (f32[4,64,512]{2,1,0:T(8,128)S(1)}, f32[4,64,512]{2,1,0:T(8,128)S(1)}) custom-call(s32[9]{0:T(128)S(1)} %dynamic-slice_bitcast_fusion.where, f32[128,1024]{1,0:T(8,128)S(1)} %get-tuple-element.162.refs_0_.refs_6_, f32[128,1024]{1,0:T(8,128)S(1)} %collective-permute-done.23.refs_1_.refs_8_, ...), custom_call_target="tpu_custom_call" | custom-call | flops 1610612736 | bytes 1048576 | tf_op jit(solution)/shard_map/gram/pallas_call | solution.py:89
  88.4 1.8 %collective-permute-start.28 = (f32[1,64,512]{2,1,0:T(8,128)S(1)}, f32[1,64,512]{2,1,0:T(8,128)S(1)}, u32[]{:S(2)}, u32[]{:S(2)}) collective-permute-start(f32[1,64,512]{2,1,0:T(8,128)S(1)} %get-tuple-element.169), channel_id=1, source_target_pairs={{0,4},{1,5},{2,6},{3,7},{4,0},{5,1},{6,2},{7,3},{8,12},{9,13},{10,... | collective-permute-start | bytes 393224 | tf_op jit(solution)/shard_map/ppermute | solution.py:237
  90.2 8.0 %collective-permute-done.27.received = f32[2,64,512]{2,1,0:T(8,128)S(1)} collective-permute-done((f32[2,64,512]{2,1,0:T(8,128)S(1)}, f32[2,64,512]{2,1,0:T(8,128)S(1)}, u32[]{:S(2)}, u32[]{:S(2)}) %collective-permute-start.27) | collective-permute-done | bytes 262176 | tf_op jit(solution)/shard_map/ppermute | solution.py:237
  99.0 2.0 %core.2.refs_13_ = f32[64,1024]{1,0:T(8,128)S(1)} custom-call(s32[9]{0:T(128)S(1)} %dynamic-slice_bitcast_fusion.where, f32[2,64,256]{2,1,0:T(8,128)S(1)} %get-tuple-element.173.refs_0_, f32[96,1024]{1,0:T(8,128)S(1)} %collective-permute-done.5.refs_1_.refs_9_, f32[96,1024]{1,0:T(8,128)S(1)} %collective-permute-done.6.refs_2_.refs_12_, ...), custom_call_target="tpu_custom_call" | custom-call | flops 402653184 | bytes 262144 | tf_op jit(solution)/shard_map/core/pallas_call | solution.py:89
  101.1 2.7 %core.3 = f32[64,1024]{1,0:T(8,128)} custom-call(s32[9]{0:T(128)S(1)} %dynamic-slice_bitcast_fusion.where, f32[2,64,256]{2,1,0:T(8,128)S(1)} %get-tuple-element.173.refs_0_, f32[96,1024]{1,0:T(8,128)S(1)} %collective-permute-done.5.refs_1_.refs_9_, f32[96,1024]{1,0:T(8,128)S(1)} %collective-permute-done.6.refs_2_.refs_12_, ...), custom_call_target="tpu_custom_call" | custom-call | flops 402653184 | bytes 262144 | tf_op jit(solution)/shard_map/core/pallas_call | solution.py:89
  103.8 2.9 %collective-permute-done.29.refs_9_ = f32[1,64,512]{2,1,0:T(8,128)S(1)} collective-permute-done((f32[1,64,512]{2,1,0:T(8,128)S(1)}, f32[1,64,512]{2,1,0:T(8,128)S(1)}, u32[]{:S(2)}, u32[]{:S(2)}) %collective-permute-start.29) | collective-permute-done | bytes 131104 | tf_op jit(solution)/shard_map/ppermute | solution.py:237
  (68 shorter events, 32.1 us)
Async XLA Ops:
  1.6 9.6 %collective-permute-start = (f32[64,1024]{1,0:T(8,128)S(1)}, f32[64,1024]{1,0:T(8,128)S(1)}, u32[]{:S(2)}, u32[]{:S(2)}) collective-permute-start(f32[64,1024]{1,0:T(8,128)S(1)} %bitcast.5), channel_id=1, source_target_pairs={{16,0},{9,1},{18,2},{11,3},{20,4},{13,5},{22,6},{15,7},{0,8},{25,9... | collective-permute-start | bytes 786440 | tf_op jit(solution)/shard_map/ppermute | solution.py:237
  4.6 8.1 %collective-permute-start.2 = (f32[64,1024]{1,0:T(8,128)S(1)}, f32[64,1024]{1,0:T(8,128)S(1)}, u32[]{:S(2)}, u32[]{:S(2)}) collective-permute-start(f32[64,1024]{1,0:T(8,128)S(1)} %bitcast.6), channel_id=1, source_target_pairs={{8,0},{17,1},{10,2},{19,3},{12,4},{21,5},{14,6},{23,7},{24,8},{1,9... | collective-permute-start | bytes 786440 | tf_op jit(solution)/shard_map/ppermute | solution.py:237
  9.2 12.4 %collective-permute-start.5 = (f32[96,1024]{1,0:T(8,128)S(1)}, f32[96,1024]{1,0:T(8,128)S(1)}, u32[]{:S(2)}, u32[]{:S(2)}) collective-permute-start(f32[96,1024]{1,0:T(8,128)S(1)} %get-tuple-element.107.refs_0_.refs_6_), channel_id=1, source_target_pairs={{16,0},{9,1},{18,2},{11,3},{20,4},{13,5},{22,6},{15,7},{0,8},{25,9... | collective-permute-start | bytes 1179656 | tf_op jit(solution)/shard_map/ppermute | solution.py:237
  11.2 8.6 %collective-permute-start.1 = (f32[64,1024]{1,0:T(8,128)S(1)}, f32[64,1024]{1,0:T(8,128)S(1)}, u32[]{:S(2)}, u32[]{:S(2)}) collective-permute-start(f32[64,1024]{1,0:T(8,128)S(1)} %collective-permute-done.refs_1_.refs_8_), channel_id=1, source_target_pairs={{16,0},{9,1},{18,2},{11,3},{20,4},{13,5},{22,6},{15,7},{0,8},{25,9... | collective-permute-start | bytes 786440 | tf_op jit(solution)/shard_map/ppermute | solution.py:237
  12.7 14.7 %collective-permute-start.11 = (f32[128,1024]{1,0:T(8,128)S(1)}, f32[128,1024]{1,0:T(8,128)S(1)}, u32[]{:S(2)}, u32[]{:S(2)}) collective-permute-start(f32[128,1024]{1,0:T(8,128)S(1)} %get-tuple-element.124.refs_0_.refs_7_), channel_id=1, source_target_pairs={{16,0},{9,1},{18,2},{11,3},{20,4},{13,5},{22,6},{15,7},{0,8},{25,9... | collective-permute-start | bytes 1572872 | tf_op jit(solution)/shard_map/ppermute | solution.py:237
  21.7 12.6 %collective-permute-start.6 = (f32[96,1024]{1,0:T(8,128)S(1)}, f32[96,1024]{1,0:T(8,128)S(1)}, u32[]{:S(2)}, u32[]{:S(2)}) collective-permute-start(f32[96,1024]{1,0:T(8,128)S(1)} %collective-permute-done.5.refs_1_.refs_9_), channel_id=1, source_target_pairs={{16,0},{9,1},{18,2},{11,3},{20,4},{13,5},{22,6},{15,7},{0,8},{25,9... | collective-permute-start | bytes 1179656 | tf_op jit(solution)/shard_map/ppermute | solution.py:237
  23.6 10.6 %collective-permute-start.7 = (f32[80,1024]{1,0:T(8,128)S(1)}, f32[80,1024]{1,0:T(8,128)S(1)}, u32[]{:S(2)}, u32[]{:S(2)}) collective-permute-start(f32[80,1024]{1,0:T(8,128)S(1)} %get-tuple-element.111), channel_id=1, source_target_pairs={{8,0},{17,1},{10,2},{19,3},{12,4},{21,5},{14,6},{23,7},{24,8},{1,9... | collective-permute-start | bytes 983048 | tf_op jit(solution)/shard_map/ppermute | solution.py:237
  25.9 21.3 %collective-permute-start.13 = (f32[128,1024]{1,0:T(8,128)S(1)}, f32[128,1024]{1,0:T(8,128)S(1)}, u32[]{:S(2)}, u32[]{:S(2)}) collective-permute-start(f32[128,1024]{1,0:T(8,128)S(1)} %get-tuple-element.124.refs_0_.refs_7_), channel_id=1, source_target_pairs={{8,0},{17,1},{10,2},{19,3},{12,4},{21,5},{14,6},{23,7},{24,8},{1,9... | collective-permute-start | bytes 1572872 | tf_op jit(solution)/shard_map/ppermute | solution.py:237
  27.4 19.8 %collective-permute-start.12 = (f32[128,1024]{1,0:T(8,128)S(1)}, f32[128,1024]{1,0:T(8,128)S(1)}, u32[]{:S(2)}, u32[]{:S(2)}) collective-permute-start(f32[128,1024]{1,0:T(8,128)S(1)} %collective-permute-done.11.refs_1_.refs_10_), channel_id=1, source_target_pairs={{16,0},{9,1},{18,2},{11,3},{20,4},{13,5},{22,6},{15,7},{0,8},{25,9... | collective-permute-start | bytes 1572872 | tf_op jit(solution)/shard_map/ppermute | solution.py:237
  37.6 6.2 %collective-permute-start.9 = (f32[2,32,512]{2,1,0:T(8,128)S(1)}, f32[2,32,512]{2,1,0:T(8,128)S(1)}, u32[]{:S(2)}, u32[]{:S(2)}) collective-permute-start(f32[2,32,512]{2,1,0:T(8,128)S(1)} %get-tuple-element.115), channel_id=1, source_target_pairs={{0,2},{1,3},{2,0},{3,1},{4,6},{5,7},{6,4},{7,5},{8,10},{9,11},{10,... | collective-permute-start | bytes 393224 | tf_op jit(solution)/shard_map/ppermute | solution.py:237
  39.3 12.0 %collective-permute-start.17 = (f32[128,1024]{1,0:T(8,128)S(1)}, f32[128,1024]{1,0:T(8,128)S(1)}, u32[]{:S(2)}, u32[]{:S(2)}) collective-permute-start(f32[128,1024]{1,0:T(8,128)S(1)} %get-tuple-element.142.refs_0_.refs_5_), channel_id=1, source_target_pairs={{16,0},{9,1},{18,2},{11,3},{20,4},{13,5},{22,6},{15,7},{0,8},{25,9... | collective-permute-start | bytes 1572872 | tf_op jit(solution)/shard_map/ppermute | solution.py:237
  49.8 13.9 %collective-permute-start.19 = (f32[128,1024]{1,0:T(8,128)S(1)}, f32[128,1024]{1,0:T(8,128)S(1)}, u32[]{:S(2)}, u32[]{:S(2)}) collective-permute-start(f32[128,1024]{1,0:T(8,128)S(1)} %get-tuple-element.142.refs_0_.refs_5_), channel_id=1, source_target_pairs={{8,0},{17,1},{10,2},{19,3},{12,4},{21,5},{14,6},{23,7},{24,8},{1,9... | collective-permute-start | bytes 1572872 | tf_op jit(solution)/shard_map/ppermute | solution.py:237
  51.3 12.9 %collective-permute-start.18 = (f32[128,1024]{1,0:T(8,128)S(1)}, f32[128,1024]{1,0:T(8,128)S(1)}, u32[]{:S(2)}, u32[]{:S(2)}) collective-permute-start(f32[128,1024]{1,0:T(8,128)S(1)} %collective-permute-done.17.refs_1_.refs_7_), channel_id=1, source_target_pairs={{16,0},{9,1},{18,2},{11,3},{20,4},{13,5},{22,6},{15,7},{0,8},{25,9... | collective-permute-start | bytes 1572872 | tf_op jit(solution)/shard_map/ppermute | solution.py:237
  52.0 9.5 %collective-permute-start.15 = (f32[2,64,512]{2,1,0:T(8,128)S(1)}, f32[2,64,512]{2,1,0:T(8,128)S(1)}, u32[]{:S(2)}, u32[]{:S(2)}) collective-permute-start(f32[2,64,512]{2,1,0:T(8,128)S(1)} %get-tuple-element.128), channel_id=1, source_target_pairs={{0,2},{1,3},{2,0},{3,1},{4,6},{5,7},{6,4},{7,5},{8,10},{9,11},{10,... | collective-permute-start | bytes 786440 | tf_op jit(solution)/shard_map/ppermute | solution.py:237
  53.7 16.0 %collective-permute-start.23 = (f32[128,1024]{1,0:T(8,128)S(1)}, f32[128,1024]{1,0:T(8,128)S(1)}, u32[]{:S(2)}, u32[]{:S(2)}) collective-permute-start(f32[128,1024]{1,0:T(8,128)S(1)} %get-tuple-element.162.refs_0_.refs_6_), channel_id=1, source_target_pairs={{16,0},{9,1},{18,2},{11,3},{20,4},{13,5},{22,6},{15,7},{0,8},{25,9... | collective-permute-start | bytes 1572872 | tf_op jit(solution)/shard_map/ppermute | solution.py:237
  55.2 6.4 %collective-permute-start.16 = (f32[1,32,512]{2,1,0:T(8,128)S(1)}, f32[1,32,512]{2,1,0:T(8,128)S(1)}, u32[]{:S(2)}, u32[]{:S(2)}) collective-permute-start(f32[1,32,512]{2,1,0:T(8,128)S(1)} %get-tuple-element.132), channel_id=1, source_target_pairs={{0,4},{1,5},{2,6},{3,7},{4,0},{5,1},{6,2},{7,3},{8,12},{9,13},{10,... | collective-permute-start | bytes 196616 | tf_op jit(solution)/shard_map/ppermute | solution.py:237
  67.4 14.9 %collective-permute-start.25 = (f32[128,1024]{1,0:T(8,128)S(1)}, f32[128,1024]{1,0:T(8,128)S(1)}, u32[]{:S(2)}, u32[]{:S(2)}) collective-permute-start(f32[128,1024]{1,0:T(8,128)S(1)} %get-tuple-element.162.refs_0_.refs_6_), channel_id=1, source_target_pairs={{8,0},{17,1},{10,2},{19,3},{12,4},{21,5},{14,6},{23,7},{24,8},{1,9... | collective-permute-start | bytes 1572872 | tf_op jit(solution)/shard_map/ppermute | solution.py:237
  69.7 12.5 %collective-permute-start.24 = (f32[128,1024]{1,0:T(8,128)S(1)}, f32[128,1024]{1,0:T(8,128)S(1)}, u32[]{:S(2)}, u32[]{:S(2)}) collective-permute-start(f32[128,1024]{1,0:T(8,128)S(1)} %collective-permute-done.23.refs_1_.refs_8_), channel_id=1, source_target_pairs={{16,0},{9,1},{18,2},{11,3},{20,4},{13,5},{22,6},{15,7},{0,8},{25,9... | collective-permute-start | bytes 1572872 | tf_op jit(solution)/shard_map/ppermute | solution.py:237
  71.5 10.6 %collective-permute-start.21 = (f32[2,64,512]{2,1,0:T(8,128)S(1)}, f32[2,64,512]{2,1,0:T(8,128)S(1)}, u32[]{:S(2)}, u32[]{:S(2)}) collective-permute-start(f32[2,64,512]{2,1,0:T(8,128)S(1)} %get-tuple-element.146), channel_id=1, source_target_pairs={{0,2},{1,3},{2,0},{3,1},{4,6},{5,7},{6,4},{7,5},{8,10},{9,11},{10,... | collective-permute-start | bytes 786440 | tf_op jit(solution)/shard_map/ppermute | solution.py:237
  72.0 10.2 %collective-permute-start.22 = (f32[1,64,512]{2,1,0:T(8,128)S(1)}, f32[1,64,512]{2,1,0:T(8,128)S(1)}, u32[]{:S(2)}, u32[]{:S(2)}) collective-permute-start(f32[1,64,512]{2,1,0:T(8,128)S(1)} %get-tuple-element.150), channel_id=1, source_target_pairs={{0,4},{1,5},{2,6},{3,7},{4,0},{5,1},{6,2},{7,3},{8,12},{9,13},{10,... | collective-permute-start | bytes 393224 | tf_op jit(solution)/shard_map/ppermute | solution.py:237
  85.1 13.9 %collective-permute-start.30 = (f32[80,1024]{1,0:T(8,128)S(1)}, f32[80,1024]{1,0:T(8,128)S(1)}, u32[]{:S(2)}, u32[]{:S(2)}) collective-permute-start(f32[80,1024]{1,0:T(8,128)S(1)} %pad_maximum_fusion), channel_id=1, source_target_pairs={{0,1},{1,0},{2,3},{3,2},{4,5},{5,4},{6,7},{7,6},{8,9},{9,8},{10,11... | collective-permute-start | bytes 983048 | tf_op jit(solution)/shard_map/ppermute | solution.py:237
  87.0 11.2 %collective-permute-start.27 = (f32[2,64,512]{2,1,0:T(8,128)S(1)}, f32[2,64,512]{2,1,0:T(8,128)S(1)}, u32[]{:S(2)}, u32[]{:S(2)}) collective-permute-start(f32[2,64,512]{2,1,0:T(8,128)S(1)} %get-tuple-element.166), channel_id=1, source_target_pairs={{0,2},{1,3},{2,0},{3,1},{4,6},{5,7},{6,4},{7,5},{8,10},{9,11},{10,... | collective-permute-start | bytes 786440 | tf_op jit(solution)/shard_map/ppermute | solution.py:237
  88.4 12.6 %collective-permute-start.28 = (f32[1,64,512]{2,1,0:T(8,128)S(1)}, f32[1,64,512]{2,1,0:T(8,128)S(1)}, u32[]{:S(2)}, u32[]{:S(2)}) collective-permute-start(f32[1,64,512]{2,1,0:T(8,128)S(1)} %get-tuple-element.169), channel_id=1, source_target_pairs={{0,4},{1,5},{2,6},{3,7},{4,0},{5,1},{6,2},{7,3},{8,12},{9,13},{10,... | collective-permute-start | bytes 393224 | tf_op jit(solution)/shard_map/ppermute | solution.py:237
  98.2 8.5 %collective-permute-start.29 = (f32[1,64,512]{2,1,0:T(8,128)S(1)}, f32[1,64,512]{2,1,0:T(8,128)S(1)}, u32[]{:S(2)}, u32[]{:S(2)}) collective-permute-start(f32[1,64,512]{2,1,0:T(8,128)S(1)} %get-tuple-element.172), channel_id=1, source_target_pairs={{0,4},{1,5},{2,6},{3,7},{4,0},{5,1},{6,2},{7,3},{8,12},{9,13},{10,... | collective-permute-start | bytes 393224 | tf_op jit(solution)/shard_map/ppermute | solution.py:237
  (9 other events, 27.1 us)

commit v4 on v3

--- a/solution.py
+++ b/solution.py
@@ -10,6 +10,7 @@
 
 AXES = ("row", "col")
 CORES = 2
+HINT = 10
 CUTS = (0, 1, 2, 4, 6, 8)
 BACK = (4, 4, 6)
 PARAMS = pltpu.CompilerParams(vmem_limit_bytes=40 * 2**20)
@@ -78,7 +79,7 @@
         out_specs=[vmem] * len(outs),
         scratch_shapes=list(scratch),
         compiler_params=PARAMS,
-        cost_estimate=pl.CostEstimate(flops=flops, bytes_accessed=4 * sum(o.size for o in outs), transcendentals=0),
+        cost_estimate=pl.CostEstimate(flops=flops // HINT, bytes_accessed=4 * sum(o.size for o in outs) // HINT, transcendentals=0),
         name=name,
     )(*args)
 
@@ -93,7 +94,7 @@
         out_specs=[vmem] * len(outs),
         scratch_shapes=list(scratch),
         compiler_params=PARAMS,
-        cost_estimate=pl.CostEstimate(flops=flops, bytes_accessed=4 * sum(o.size for o in outs), transcendentals=0),
+        cost_estimate=pl.CostEstimate(flops=flops // HINT, bytes_accessed=4 * sum(o.size for o in outs) // HINT, transcendentals=0),
         name=name,
     )(*args)
 

time: 108 us -> 107 us (level)
  waiting for transfers between devices: 44.3 us -> 40.6 us
  starting transfers between devices: 39.7 us -> 42.4 us
    ppermute x31, waiting for transfers between devices: 44.3 us -> 40.6 us  [send(): return lax.ppermute(value, AXES, pairs)]
    ppermute x31, starting transfers between devices: 39.7 us -> 42.4 us  [send(): return lax.ppermute(value, AXES, pairs)]
  transfers between devices with their start and end apart: 31 -> 31, of which waited for: 13 -> 16; matrix products, arithmetic and copies ran while one was open for 1% -> 1% of each run, Pallas kernels for 14% -> 14%
where the time goes in v4:
time: 107 us; the launch traced here: 106 us
  starting transfers between devices  42.4 us (40%)
  waiting for transfers between devices  40.6 us (38%)
  Pallas kernels  18.2 us (17%)
  local copies, waits for them, and re-layouts  4.32 us (4%)
    ppermute x31, starting transfers between devices, send(): return lax.ppermute(value, AXES, pairs)  42.4 us
    ppermute x31, waiting for transfers between devices, send(): return lax.ppermute(value, AXES, pairs)  40.6 us
    pallas_call x20, Pallas kernels, call(): pl.pallas_call(kernel, out_shape=outs, in_specs=specs, out_specs=[vmem] *...  18.2 us
    unnamed x4, local copies, waits for them, and re-layouts  2.63 us
  transfers between devices with their start and end apart: 31, of which 16 were waited for; matrix products, arithmetic and copies ran while one was open for 1% of the time, Pallas kernels for 14%

profile of v4, /device:TPU:0, one launch (start us, length us, event | category | flops | bytes accessed | tf_op | source)
XLA Modules:
  0.0 106.4 jit_solution(1696266395674363260)
XLA Ops:
  1.6 3.0 %collective-permute-start = (f32[64,1024]{1,0:T(8,128)S(1)}, f32[64,1024]{1,0:T(8,128)S(1)}, u32[]{:S(2)}, u32[]{:S(2)}) collective-permute-start(f32[64,1024]{1,0:T(8,128)S(1)} %bitcast.5), channel_id=1, source_target_pairs={{16,0},{9,1},{18,2},{11,3},{20,4},{13,5},{22,6},{15,7},{0,8},{25,9... | collective-permute-start | bytes 786440 | tf_op jit(solution)/shard_map/ppermute | solution.py:238
  9.2 2.0 %collective-permute-start.5 = (f32[96,1024]{1,0:T(8,128)S(1)}, f32[96,1024]{1,0:T(8,128)S(1)}, u32[]{:S(2)}, u32[]{:S(2)}) collective-permute-start(f32[96,1024]{1,0:T(8,128)S(1)} %get-tuple-element.107.refs_0_.refs_6_), channel_id=1, source_target_pairs={{16,0},{9,1},{18,2},{11,3},{20,4},{13,5},{22,6},{15,7},{0,8},{25,9... | collective-permute-start | bytes 1179656 | tf_op jit(solution)/shard_map/ppermute | solution.py:238
  14.4 5.5 %collective-permute-done.1.refs_2_.refs_11_ = f32[64,1024]{1,0:T(8,128)S(1)} collective-permute-done((f32[64,1024]{1,0:T(8,128)S(1)}, f32[64,1024]{1,0:T(8,128)S(1)}, u32[]{:S(2)}, u32[]{:S(2)}) %collective-permute-start.1) | collective-permute-done | bytes 262176 | tf_op jit(solution)/shard_map/ppermute | solution.py:238
  21.6 2.0 %collective-permute-start.6 = (f32[96,1024]{1,0:T(8,128)S(1)}, f32[96,1024]{1,0:T(8,128)S(1)}, u32[]{:S(2)}, u32[]{:S(2)}) collective-permute-start(f32[96,1024]{1,0:T(8,128)S(1)} %collective-permute-done.5.refs_1_.refs_9_), channel_id=1, source_target_pairs={{16,0},{9,1},{18,2},{11,3},{20,4},{13,5},{22,6},{15,7},{0,8},{25,9... | collective-permute-start | bytes 1179656 | tf_op jit(solution)/shard_map/ppermute | solution.py:238
  23.8 2.1 %collective-permute-start.4 = (f32[2,32,512]{2,1,0:T(8,128)S(1)}, f32[2,32,512]{2,1,0:T(8,128)S(1)}, u32[]{:S(2)}, u32[]{:S(2)}) collective-permute-start(f32[2,32,512]{2,1,0:T(8,128)S(1)} %get-tuple-element.104), channel_id=1, source_target_pairs={{0,2},{1,3},{2,0},{3,1},{4,6},{5,7},{6,4},{7,5},{8,10},{9,11},{10,... | collective-permute-start | bytes 393224 | tf_op jit(solution)/shard_map/ppermute | solution.py:238
  29.4 4.9 %collective-permute-done.7.refs_3_.refs_15_ = f32[80,1024]{1,0:T(8,128)S(1)} collective-permute-done((f32[80,1024]{1,0:T(8,128)S(1)}, f32[80,1024]{1,0:T(8,128)S(1)}, u32[]{:S(2)}, u32[]{:S(2)}) %collective-permute-start.7) | collective-permute-done | bytes 327712 | tf_op jit(solution)/shard_map/ppermute | solution.py:238
  36.1 2.3 %collective-permute-start.17 = (f32[128,1024]{1,0:T(8,128)S(1)}, f32[128,1024]{1,0:T(8,128)S(1)}, u32[]{:S(2)}, u32[]{:S(2)}) collective-permute-start(f32[128,1024]{1,0:T(8,128)S(1)} %get-tuple-element.142.refs_0_.refs_5_), channel_id=1, source_target_pairs={{16,0},{9,1},{18,2},{11,3},{20,4},{13,5},{22,6},{15,7},{0,8},{25,9... | collective-permute-start | bytes 1572872 | tf_op jit(solution)/shard_map/ppermute | solution.py:238
  39.8 2.6 %collective-permute-start.10 = (f32[1,32,512]{2,1,0:T(8,128)S(1)}, f32[1,32,512]{2,1,0:T(8,128)S(1)}, u32[]{:S(2)}, u32[]{:S(2)}) collective-permute-start(f32[1,32,512]{2,1,0:T(8,128)S(1)} %get-tuple-element.119), channel_id=1, source_target_pairs={{0,4},{1,5},{2,6},{3,7},{4,0},{5,1},{6,2},{7,3},{8,12},{9,13},{10,... | collective-permute-start | bytes 196616 | tf_op jit(solution)/shard_map/ppermute | solution.py:238
  45.5 2.5 %gram.7 = (f32[4,64,512]{2,1,0:T(8,128)S(1)}, f32[4,64,512]{2,1,0:T(8,128)S(1)}) custom-call(s32[9]{0:T(128)S(1)} %dynamic-slice_bitcast_fusion.where, f32[128,1024]{1,0:T(8,128)S(1)} %get-tuple-element.124.refs_0_.refs_7_, f32[128,1024]{1,0:T(8,128)S(1)} %collective-permute-done.11.refs_1_.refs_10_, ...), custom_call_target="tpu_custom_call" | custom-call | flops 161061280 | bytes 104857 | tf_op jit(solution)/shard_map/gram/pallas_call | solution.py:90
  50.0 1.9 %collective-permute-start.18 = (f32[128,1024]{1,0:T(8,128)S(1)}, f32[128,1024]{1,0:T(8,128)S(1)}, u32[]{:S(2)}, u32[]{:S(2)}) collective-permute-start(f32[128,1024]{1,0:T(8,128)S(1)} %collective-permute-done.17.refs_1_.refs_7_), channel_id=1, source_target_pairs={{16,0},{9,1},{18,2},{11,3},{20,4},{13,5},{22,6},{15,7},{0,8},{25,9... | collective-permute-start | bytes 1572872 | tf_op jit(solution)/shard_map/ppermute | solution.py:238
  55.2 2.6 %collective-permute-start.16 = (f32[1,32,512]{2,1,0:T(8,128)S(1)}, f32[1,32,512]{2,1,0:T(8,128)S(1)}, u32[]{:S(2)}, u32[]{:S(2)}) collective-permute-start(f32[1,32,512]{2,1,0:T(8,128)S(1)} %get-tuple-element.132), channel_id=1, source_target_pairs={{0,4},{1,5},{2,6},{3,7},{4,0},{5,1},{6,2},{7,3},{8,12},{9,13},{10,... | collective-permute-start | bytes 196616 | tf_op jit(solution)/shard_map/ppermute | solution.py:238
  57.8 2.8 %collective-permute-done.15.received = f32[2,64,512]{2,1,0:T(8,128)S(1)} collective-permute-done((f32[2,64,512]{2,1,0:T(8,128)S(1)}, f32[2,64,512]{2,1,0:T(8,128)S(1)}, u32[]{:S(2)}, u32[]{:S(2)}) %collective-permute-start.15) | collective-permute-done | bytes 262176 | tf_op jit(solution)/shard_map/ppermute | solution.py:238
  62.5 2.5 %gram.8 = (f32[4,64,512]{2,1,0:T(8,128)S(1)}, f32[4,64,512]{2,1,0:T(8,128)S(1)}) custom-call(s32[9]{0:T(128)S(1)} %dynamic-slice_bitcast_fusion.where, f32[128,1024]{1,0:T(8,128)S(1)} %get-tuple-element.142.refs_0_.refs_5_, f32[128,1024]{1,0:T(8,128)S(1)} %collective-permute-done.17.refs_1_.refs_7_, f32[128,1024]{1,0:T(8,128)S(1)} %collective-permute-done.18.refs_2_.refs_9_, ...), custom_call_target="tpu_custom_call" | custom-call | flops 161061280 | bytes 104857 | tf_op jit(solution)/shard_map/gram/pallas_call | solution.py:90
  69.7 2.2 %collective-permute-start.21 = (f32[2,64,512]{2,1,0:T(8,128)S(1)}, f32[2,64,512]{2,1,0:T(8,128)S(1)}, u32[]{:S(2)}, u32[]{:S(2)}) collective-permute-start(f32[2,64,512]{2,1,0:T(8,128)S(1)} %get-tuple-element.146), channel_id=1, source_target_pairs={{0,2},{1,3},{2,0},{3,1},{4,6},{5,7},{6,4},{7,5},{8,10},{9,11},{10,... | collective-permute-start | bytes 786440 | tf_op jit(solution)/shard_map/ppermute | solution.py:238
  71.9 2.0 %collective-permute-start.22 = (f32[1,64,512]{2,1,0:T(8,128)S(1)}, f32[1,64,512]{2,1,0:T(8,128)S(1)}, u32[]{:S(2)}, u32[]{:S(2)}) collective-permute-start(f32[1,64,512]{2,1,0:T(8,128)S(1)} %get-tuple-element.150), channel_id=1, source_target_pairs={{0,4},{1,5},{2,6},{3,7},{4,0},{5,1},{6,2},{7,3},{8,12},{9,13},{10,... | collective-permute-start | bytes 393224 | tf_op jit(solution)/shard_map/ppermute | solution.py:238
  73.9 7.1 %collective-permute-done.21.received = f32[2,64,512]{2,1,0:T(8,128)S(1)} collective-permute-done((f32[2,64,512]{2,1,0:T(8,128)S(1)}, f32[2,64,512]{2,1,0:T(8,128)S(1)}, u32[]{:S(2)}, u32[]{:S(2)}) %collective-permute-start.21) | collective-permute-done | bytes 262176 | tf_op jit(solution)/shard_map/ppermute | solution.py:238
  81.1 2.7 %gram.9 = (f32[4,64,512]{2,1,0:T(8,128)S(1)}, f32[4,64,512]{2,1,0:T(8,128)S(1)}) custom-call(s32[9]{0:T(128)S(1)} %dynamic-slice_bitcast_fusion.where, f32[128,1024]{1,0:T(8,128)S(1)} %get-tuple-element.162.refs_0_.refs_6_, f32[128,1024]{1,0:T(8,128)S(1)} %collective-permute-done.23.refs_1_.refs_8_, ...), custom_call_target="tpu_custom_call" | custom-call | flops 161061280 | bytes 104857 | tf_op jit(solution)/shard_map/gram/pallas_call | solution.py:90
  83.9 1.8 %collective-permute-done.26.received = f32[4,64,512]{2,1,0:T(8,128)S(1)} collective-permute-done((f32[4,64,512]{2,1,0:T(8,128)S(1)}, f32[4,64,512]{2,1,0:T(8,128)S(1)}, u32[]{:S(2)}, u32[]{:S(2)}) %collective-permute-start.26) | collective-permute-done | bytes 524320 | tf_op jit(solution)/shard_map/ppermute | solution.py:238
  85.8 1.8 %collective-permute-start.27 = (f32[2,64,512]{2,1,0:T(8,128)S(1)}, f32[2,64,512]{2,1,0:T(8,128)S(1)}, u32[]{:S(2)}, u32[]{:S(2)}) collective-permute-start(f32[2,64,512]{2,1,0:T(8,128)S(1)} %get-tuple-element.166), channel_id=1, source_target_pairs={{0,2},{1,3},{2,0},{3,1},{4,6},{5,7},{6,4},{7,5},{8,10},{9,11},{10,... | collective-permute-start | bytes 786440 | tf_op jit(solution)/shard_map/ppermute | solution.py:238
  87.7 1.9 %collective-permute-start.28 = (f32[1,64,512]{2,1,0:T(8,128)S(1)}, f32[1,64,512]{2,1,0:T(8,128)S(1)}, u32[]{:S(2)}, u32[]{:S(2)}) collective-permute-start(f32[1,64,512]{2,1,0:T(8,128)S(1)} %get-tuple-element.169), channel_id=1, source_target_pairs={{0,4},{1,5},{2,6},{3,7},{4,0},{5,1},{6,2},{7,3},{8,12},{9,13},{10,... | collective-permute-start | bytes 393224 | tf_op jit(solution)/shard_map/ppermute | solution.py:238
  89.6 7.5 %collective-permute-done.27.received = f32[2,64,512]{2,1,0:T(8,128)S(1)} collective-permute-done((f32[2,64,512]{2,1,0:T(8,128)S(1)}, f32[2,64,512]{2,1,0:T(8,128)S(1)}, u32[]{:S(2)}, u32[]{:S(2)}) %collective-permute-start.27) | collective-permute-done | bytes 262176 | tf_op jit(solution)/shard_map/ppermute | solution.py:238
  98.2 1.9 %core.2.refs_13_ = f32[64,1024]{1,0:T(8,128)S(1)} custom-call(s32[9]{0:T(128)S(1)} %dynamic-slice_bitcast_fusion.where, f32[2,64,256]{2,1,0:T(8,128)S(1)} %get-tuple-element.173.refs_0_, f32[96,1024]{1,0:T(8,128)S(1)} %collective-permute-done.5.refs_1_.refs_9_, f32[96,1024]{1,0:T(8,128)S(1)} %collective-permute-done.6.refs_2_.refs_12_, ...), custom_call_target="tpu_custom_call" | custom-call | flops 40265320 | bytes 26214 | tf_op jit(solution)/shard_map/core/pallas_call | solution.py:90
  100.1 2.7 %core.3 = f32[64,1024]{1,0:T(8,128)} custom-call(s32[9]{0:T(128)S(1)} %dynamic-slice_bitcast_fusion.where, f32[2,64,256]{2,1,0:T(8,128)S(1)} %get-tuple-element.173.refs_0_, f32[96,1024]{1,0:T(8,128)S(1)} %collective-permute-done.5.refs_1_.refs_9_, f32[96,1024]{1,0:T(8,128)S(1)} %collective-permute-done.6.refs_2_.refs_12_, ...), custom_call_target="tpu_custom_call" | custom-call | flops 40265320 | bytes 26214 | tf_op jit(solution)/shard_map/core/pallas_call | solution.py:90
  102.8 2.7 %collective-permute-done.29.refs_9_ = f32[1,64,512]{2,1,0:T(8,128)S(1)} collective-permute-done((f32[1,64,512]{2,1,0:T(8,128)S(1)}, f32[1,64,512]{2,1,0:T(8,128)S(1)}, u32[]{:S(2)}, u32[]{:S(2)}) %collective-permute-start.29) | collective-permute-done | bytes 131104 | tf_op jit(solution)/shard_map/ppermute | solution.py:238
  (68 shorter events, 34.6 us)
Async XLA Ops:
  1.6 9.6 %collective-permute-start = (f32[64,1024]{1,0:T(8,128)S(1)}, f32[64,1024]{1,0:T(8,128)S(1)}, u32[]{:S(2)}, u32[]{:S(2)}) collective-permute-start(f32[64,1024]{1,0:T(8,128)S(1)} %bitcast.5), channel_id=1, source_target_pairs={{16,0},{9,1},{18,2},{11,3},{20,4},{13,5},{22,6},{15,7},{0,8},{25,9... | collective-permute-start | bytes 786440 | tf_op jit(solution)/shard_map/ppermute | solution.py:238
  4.6 8.1 %collective-permute-start.2 = (f32[64,1024]{1,0:T(8,128)S(1)}, f32[64,1024]{1,0:T(8,128)S(1)}, u32[]{:S(2)}, u32[]{:S(2)}) collective-permute-start(f32[64,1024]{1,0:T(8,128)S(1)} %bitcast.6), channel_id=1, source_target_pairs={{8,0},{17,1},{10,2},{19,3},{12,4},{21,5},{14,6},{23,7},{24,8},{1,9... | collective-permute-start | bytes 786440 | tf_op jit(solution)/shard_map/ppermute | solution.py:238
  9.2 12.4 %collective-permute-start.5 = (f32[96,1024]{1,0:T(8,128)S(1)}, f32[96,1024]{1,0:T(8,128)S(1)}, u32[]{:S(2)}, u32[]{:S(2)}) collective-permute-start(f32[96,1024]{1,0:T(8,128)S(1)} %get-tuple-element.107.refs_0_.refs_6_), channel_id=1, source_target_pairs={{16,0},{9,1},{18,2},{11,3},{20,4},{13,5},{22,6},{15,7},{0,8},{25,9... | collective-permute-start | bytes 1179656 | tf_op jit(solution)/shard_map/ppermute | solution.py:238
  11.2 8.6 %collective-permute-start.1 = (f32[64,1024]{1,0:T(8,128)S(1)}, f32[64,1024]{1,0:T(8,128)S(1)}, u32[]{:S(2)}, u32[]{:S(2)}) collective-permute-start(f32[64,1024]{1,0:T(8,128)S(1)} %collective-permute-done.refs_1_.refs_8_), channel_id=1, source_target_pairs={{16,0},{9,1},{18,2},{11,3},{20,4},{13,5},{22,6},{15,7},{0,8},{25,9... | collective-permute-start | bytes 786440 | tf_op jit(solution)/shard_map/ppermute | solution.py:238
  12.7 14.6 %collective-permute-start.11 = (f32[128,1024]{1,0:T(8,128)S(1)}, f32[128,1024]{1,0:T(8,128)S(1)}, u32[]{:S(2)}, u32[]{:S(2)}) collective-permute-start(f32[128,1024]{1,0:T(8,128)S(1)} %get-tuple-element.124.refs_0_.refs_7_), channel_id=1, source_target_pairs={{16,0},{9,1},{18,2},{11,3},{20,4},{13,5},{22,6},{15,7},{0,8},{25,9... | collective-permute-start | bytes 1572872 | tf_op jit(solution)/shard_map/ppermute | solution.py:238
  21.6 12.6 %collective-permute-start.6 = (f32[96,1024]{1,0:T(8,128)S(1)}, f32[96,1024]{1,0:T(8,128)S(1)}, u32[]{:S(2)}, u32[]{:S(2)}) collective-permute-start(f32[96,1024]{1,0:T(8,128)S(1)} %collective-permute-done.5.refs_1_.refs_9_), channel_id=1, source_target_pairs={{16,0},{9,1},{18,2},{11,3},{20,4},{13,5},{22,6},{15,7},{0,8},{25,9... | collective-permute-start | bytes 1179656 | tf_op jit(solution)/shard_map/ppermute | solution.py:238
  23.6 10.6 %collective-permute-start.7 = (f32[80,1024]{1,0:T(8,128)S(1)}, f32[80,1024]{1,0:T(8,128)S(1)}, u32[]{:S(2)}, u32[]{:S(2)}) collective-permute-start(f32[80,1024]{1,0:T(8,128)S(1)} %get-tuple-element.111), channel_id=1, source_target_pairs={{8,0},{17,1},{10,2},{19,3},{12,4},{21,5},{14,6},{23,7},{24,8},{1,9... | collective-permute-start | bytes 983048 | tf_op jit(solution)/shard_map/ppermute | solution.py:238
  25.8 19.7 %collective-permute-start.13 = (f32[128,1024]{1,0:T(8,128)S(1)}, f32[128,1024]{1,0:T(8,128)S(1)}, u32[]{:S(2)}, u32[]{:S(2)}) collective-permute-start(f32[128,1024]{1,0:T(8,128)S(1)} %get-tuple-element.124.refs_0_.refs_7_), channel_id=1, source_target_pairs={{8,0},{17,1},{10,2},{19,3},{12,4},{21,5},{14,6},{23,7},{24,8},{1,9... | collective-permute-start | bytes 1572872 | tf_op jit(solution)/shard_map/ppermute | solution.py:238
  27.4 18.1 %collective-permute-start.12 = (f32[128,1024]{1,0:T(8,128)S(1)}, f32[128,1024]{1,0:T(8,128)S(1)}, u32[]{:S(2)}, u32[]{:S(2)}) collective-permute-start(f32[128,1024]{1,0:T(8,128)S(1)} %collective-permute-done.11.refs_1_.refs_10_), channel_id=1, source_target_pairs={{16,0},{9,1},{18,2},{11,3},{20,4},{13,5},{22,6},{15,7},{0,8},{25,9... | collective-permute-start | bytes 1572872 | tf_op jit(solution)/shard_map/ppermute | solution.py:238
  36.1 14.0 %collective-permute-start.17 = (f32[128,1024]{1,0:T(8,128)S(1)}, f32[128,1024]{1,0:T(8,128)S(1)}, u32[]{:S(2)}, u32[]{:S(2)}) collective-permute-start(f32[128,1024]{1,0:T(8,128)S(1)} %get-tuple-element.142.refs_0_.refs_5_), channel_id=1, source_target_pairs={{16,0},{9,1},{18,2},{11,3},{20,4},{13,5},{22,6},{15,7},{0,8},{25,9... | collective-permute-start | bytes 1572872 | tf_op jit(solution)/shard_map/ppermute | solution.py:238
  38.3 5.7 %collective-permute-start.9 = (f32[2,32,512]{2,1,0:T(8,128)S(1)}, f32[2,32,512]{2,1,0:T(8,128)S(1)}, u32[]{:S(2)}, u32[]{:S(2)}) collective-permute-start(f32[2,32,512]{2,1,0:T(8,128)S(1)} %get-tuple-element.115), channel_id=1, source_target_pairs={{0,2},{1,3},{2,0},{3,1},{4,6},{5,7},{6,4},{7,5},{8,10},{9,11},{10,... | collective-permute-start | bytes 393224 | tf_op jit(solution)/shard_map/ppermute | solution.py:238
  48.1 14.2 %collective-permute-start.19 = (f32[128,1024]{1,0:T(8,128)S(1)}, f32[128,1024]{1,0:T(8,128)S(1)}, u32[]{:S(2)}, u32[]{:S(2)}) collective-permute-start(f32[128,1024]{1,0:T(8,128)S(1)} %get-tuple-element.142.refs_0_.refs_5_), channel_id=1, source_target_pairs={{8,0},{17,1},{10,2},{19,3},{12,4},{21,5},{14,6},{23,7},{24,8},{1,9... | collective-permute-start | bytes 1572872 | tf_op jit(solution)/shard_map/ppermute | solution.py:238
  50.0 12.4 %collective-permute-start.18 = (f32[128,1024]{1,0:T(8,128)S(1)}, f32[128,1024]{1,0:T(8,128)S(1)}, u32[]{:S(2)}, u32[]{:S(2)}) collective-permute-start(f32[128,1024]{1,0:T(8,128)S(1)} %collective-permute-done.17.refs_1_.refs_7_), channel_id=1, source_target_pairs={{16,0},{9,1},{18,2},{11,3},{20,4},{13,5},{22,6},{15,7},{0,8},{25,9... | collective-permute-start | bytes 1572872 | tf_op jit(solution)/shard_map/ppermute | solution.py:238
  52.0 8.6 %collective-permute-start.15 = (f32[2,64,512]{2,1,0:T(8,128)S(1)}, f32[2,64,512]{2,1,0:T(8,128)S(1)}, u32[]{:S(2)}, u32[]{:S(2)}) collective-permute-start(f32[2,64,512]{2,1,0:T(8,128)S(1)} %get-tuple-element.128), channel_id=1, source_target_pairs={{0,2},{1,3},{2,0},{3,1},{4,6},{5,7},{6,4},{7,5},{8,10},{9,11},{10,... | collective-permute-start | bytes 786440 | tf_op jit(solution)/shard_map/ppermute | solution.py:238
  53.7 14.4 %collective-permute-start.23 = (f32[128,1024]{1,0:T(8,128)S(1)}, f32[128,1024]{1,0:T(8,128)S(1)}, u32[]{:S(2)}, u32[]{:S(2)}) collective-permute-start(f32[128,1024]{1,0:T(8,128)S(1)} %get-tuple-element.162.refs_0_.refs_6_), channel_id=1, source_target_pairs={{16,0},{9,1},{18,2},{11,3},{20,4},{13,5},{22,6},{15,7},{0,8},{25,9... | collective-permute-start | bytes 1572872 | tf_op jit(solution)/shard_map/ppermute | solution.py:238
  55.2 5.8 %collective-permute-start.16 = (f32[1,32,512]{2,1,0:T(8,128)S(1)}, f32[1,32,512]{2,1,0:T(8,128)S(1)}, u32[]{:S(2)}, u32[]{:S(2)}) collective-permute-start(f32[1,32,512]{2,1,0:T(8,128)S(1)} %get-tuple-element.132), channel_id=1, source_target_pairs={{0,4},{1,5},{2,6},{3,7},{4,0},{5,1},{6,2},{7,3},{8,12},{9,13},{10,... | collective-permute-start | bytes 196616 | tf_op jit(solution)/shard_map/ppermute | solution.py:238
  65.7 15.3 %collective-permute-start.25 = (f32[128,1024]{1,0:T(8,128)S(1)}, f32[128,1024]{1,0:T(8,128)S(1)}, u32[]{:S(2)}, u32[]{:S(2)}) collective-permute-start(f32[128,1024]{1,0:T(8,128)S(1)} %get-tuple-element.162.refs_0_.refs_6_), channel_id=1, source_target_pairs={{8,0},{17,1},{10,2},{19,3},{12,4},{21,5},{14,6},{23,7},{24,8},{1,9... | collective-permute-start | bytes 1572872 | tf_op jit(solution)/shard_map/ppermute | solution.py:238
  68.1 13.0 %collective-permute-start.24 = (f32[128,1024]{1,0:T(8,128)S(1)}, f32[128,1024]{1,0:T(8,128)S(1)}, u32[]{:S(2)}, u32[]{:S(2)}) collective-permute-start(f32[128,1024]{1,0:T(8,128)S(1)} %collective-permute-done.23.refs_1_.refs_8_), channel_id=1, source_target_pairs={{16,0},{9,1},{18,2},{11,3},{20,4},{13,5},{22,6},{15,7},{0,8},{25,9... | collective-permute-start | bytes 1572872 | tf_op jit(solution)/shard_map/ppermute | solution.py:238
  69.7 11.3 %collective-permute-start.21 = (f32[2,64,512]{2,1,0:T(8,128)S(1)}, f32[2,64,512]{2,1,0:T(8,128)S(1)}, u32[]{:S(2)}, u32[]{:S(2)}) collective-permute-start(f32[2,64,512]{2,1,0:T(8,128)S(1)} %get-tuple-element.146), channel_id=1, source_target_pairs={{0,2},{1,3},{2,0},{3,1},{4,6},{5,7},{6,4},{7,5},{8,10},{9,11},{10,... | collective-permute-start | bytes 786440 | tf_op jit(solution)/shard_map/ppermute | solution.py:238
  71.9 9.1 %collective-permute-start.22 = (f32[1,64,512]{2,1,0:T(8,128)S(1)}, f32[1,64,512]{2,1,0:T(8,128)S(1)}, u32[]{:S(2)}, u32[]{:S(2)}) collective-permute-start(f32[1,64,512]{2,1,0:T(8,128)S(1)} %get-tuple-element.150), channel_id=1, source_target_pairs={{0,4},{1,5},{2,6},{3,7},{4,0},{5,1},{6,2},{7,3},{8,12},{9,13},{10,... | collective-permute-start | bytes 393224 | tf_op jit(solution)/shard_map/ppermute | solution.py:238
  85.8 11.2 %collective-permute-start.27 = (f32[2,64,512]{2,1,0:T(8,128)S(1)}, f32[2,64,512]{2,1,0:T(8,128)S(1)}, u32[]{:S(2)}, u32[]{:S(2)}) collective-permute-start(f32[2,64,512]{2,1,0:T(8,128)S(1)} %get-tuple-element.166), channel_id=1, source_target_pairs={{0,2},{1,3},{2,0},{3,1},{4,6},{5,7},{6,4},{7,5},{8,10},{9,11},{10,... | collective-permute-start | bytes 786440 | tf_op jit(solution)/shard_map/ppermute | solution.py:238
  87.6 10.6 %collective-permute-start.30 = (f32[80,1024]{1,0:T(8,128)S(1)}, f32[80,1024]{1,0:T(8,128)S(1)}, u32[]{:S(2)}, u32[]{:S(2)}) collective-permute-start(f32[80,1024]{1,0:T(8,128)S(1)} %pad_maximum_fusion), channel_id=1, source_target_pairs={{0,1},{1,0},{2,3},{3,2},{4,5},{5,4},{6,7},{7,6},{8,9},{9,8},{10,11... | collective-permute-start | bytes 983048 | tf_op jit(solution)/shard_map/ppermute | solution.py:238
  87.7 12.4 %collective-permute-start.28 = (f32[1,64,512]{2,1,0:T(8,128)S(1)}, f32[1,64,512]{2,1,0:T(8,128)S(1)}, u32[]{:S(2)}, u32[]{:S(2)}) collective-permute-start(f32[1,64,512]{2,1,0:T(8,128)S(1)} %get-tuple-element.169), channel_id=1, source_target_pairs={{0,4},{1,5},{2,6},{3,7},{4,0},{5,1},{6,2},{7,3},{8,12},{9,13},{10,... | collective-permute-start | bytes 393224 | tf_op jit(solution)/shard_map/ppermute | solution.py:238
  97.1 8.5 %collective-permute-start.29 = (f32[1,64,512]{2,1,0:T(8,128)S(1)}, f32[1,64,512]{2,1,0:T(8,128)S(1)}, u32[]{:S(2)}, u32[]{:S(2)}) collective-permute-start(f32[1,64,512]{2,1,0:T(8,128)S(1)} %get-tuple-element.172), channel_id=1, source_target_pairs={{0,4},{1,5},{2,6},{3,7},{4,0},{5,1},{6,2},{7,3},{8,12},{9,13},{10,... | collective-permute-start | bytes 393224 | tf_op jit(solution)/shard_map/ppermute | solution.py:238
  (9 other events, 28.9 us)
